TPU v7x, 128 devices: a whole 4x4x4 slice. The times are simulated.
128 devices in a mesh: row: 16 (over x, y), col: 8 (over z, core).
Axes of the slice: x: 4, y: 4, z: 4, core: 2. Of those that a mesh axis runs over, the one named last changes fastest.
Arguments:
- pair: bfloat16 [640, 640, 128], P('row', 'col'), may hold values from -6 to 6
- pair_mask: int32 [640, 640], P('row', 'col'), may hold values 0 or 1
- node_state: float32 [640, 64], P('row'), may hold values from -6 to 6
- coords: float32 [3, 640], P(None, 'row'), may hold values from -40 to 40
- neighbours: int32 [640, 64], P('row'), may hold values from 0 to 639
- atom_type: int32 [640], P('row'), may hold values from 0 to 79
- type_table: float32 [80, 64], replicated, may hold values from -4 to 4
- node_query: float32 [64, 64], replicated, may hold values from -0.75 to 0.75
- node_key: float32 [64, 64], replicated, may hold values from -0.75 to 0.75
- node_value: float32 [64, 64], replicated, may hold values from -0.75 to 0.75
- edge_pair: bfloat16 [128, 128], replicated, may hold values from -0.5 to 0.5
- edge_radial: float32 [64, 128], replicated, may hold values from -4 to 49
- node_out_w: float32 [64, 64], replicated, may hold values from -0.75 to 0.75
- coord_gain: float32 [4], replicated, may hold values from 0.02 to 0.12
- radial_pair: float32 [64, 128], replicated, may hold values from -4 to 4
- row_gain: float32 [128], replicated, may hold values from 0.5 to 1.5
- row_query: bfloat16 [128, 128], replicated, may hold values from -1 to 1
- row_key: bfloat16 [128, 128], replicated, may hold values from -1 to 1
- row_value: bfloat16 [128, 128], replicated, may hold values from -1.75 to 1.75
- row_gate: bfloat16 [128, 128], replicated, may hold values from -0.5 to 0.5
- row_out: bfloat16 [128, 128], replicated, may hold values from -1.75 to 1.75
- row_bias: float32 [64, 4], replicated, may hold values from -8 to 143
- column_gain: float32 [128], replicated, may hold values from 0.5 to 1.5
- column_query: bfloat16 [128, 128], replicated, may hold values from -1 to 1
- column_key: bfloat16 [128, 128], replicated, may hold values from -1 to 1
- column_value: bfloat16 [128, 128], replicated, may hold values from -1 to 1
- column_gate: bfloat16 [128, 128], replicated, may hold values from -0.5 to 0.5
- column_out: bfloat16 [128, 128], replicated, may hold values from -1 to 1
- column_bias: float32 [64, 4], replicated, may hold values from -8 to 143
Outputs:
- pair_out: bfloat16 [640, 640, 128], P('row', 'col')
- node_out: float32 [640, 64], P('row')
- coords_out: float32 [3, 640], P(None, 'row')
Inputs may be any that keep to these rules, and one draw needn't show every extreme that they name: `neighbours`: token indices. `atom_type`: type indices.
All inputs are finite; a program needn't handle non-finite values. No bound on the sum of `pair_mask` on one device may be relied on, other than what follows from the above.
Results may differ from a plain program's by a relative error of at most 0.034.
Values may be sent and summed in bfloat16 or wider, within the bound.
No kernel may reach another device: no remote copies, remote signals or barrier semaphores. Data moves between devices by JAX's collectives and lax.ppermute only.
A program may use at most 128 MiB of HBM per device.

v0:
```python
import math

import jax
import jax.numpy as jnp
from jax import lax
from jax.sharding import PartitionSpec as P

PRECISE = lax.Precision.HIGHEST
RADIAL_REACH = 24.0
NEGATIVE = -1e30


def combined_all(x, axis, combine):
    everything = jax.tree.map(lambda part: lax.all_gather(part, axis), x)
    leading = jax.tree.map(lambda part: part[0], everything)

    def lap(k, so_far):
        return combine(so_far, jax.tree.map(lambda part: part[k], everything))

    return lax.fori_loop(1, lax.axis_size(axis), lap, leading)


def radial(spacing, bins):
    centers = jnp.arange(bins, dtype=jnp.float32) * (RADIAL_REACH / (bins - 1))
    spread_width = RADIAL_REACH / bins
    return jnp.exp(-jnp.square((spacing[..., None] - centers) / spread_width))


def distances(near_xyz, far_xyz):
    displacement = near_xyz[:, :, None] - far_xyz[:, None, :]
    return jnp.sqrt(jnp.sum(displacement * displacement, axis=0) + 1e-06)


def pair_bias(near_xyz, far_xyz, weight_bias):
    far_count = far_xyz.shape[1]
    block_size = math.gcd(far_count, 128)
    blocks = far_xyz.reshape(3, far_count // block_size, block_size).transpose(1, 0, 2)

    def one_block(column_xyz):
        features = radial(distances(near_xyz, column_xyz), weight_bias.shape[0])
        return jnp.einsum("abr,rh->hab", features, weight_bias, precision=PRECISE)

    stacked = lax.map(one_block, blocks)
    return stacked.transpose(1, 2, 0, 3).reshape(weight_bias.shape[1], near_xyz.shape[1], far_count)


def layer_norm(values, norm_gain):
    values = values.astype(jnp.float32)
    center = jnp.mean(values, axis=-1, keepdims=True)
    spread = jnp.mean(jnp.square(values - center), axis=-1, keepdims=True)
    return (values - center) * lax.rsqrt(spread + 1e-05) * norm_gain


def softmax_last(logits):
    highest = jnp.max(logits, axis=-1, keepdims=True)
    scaled = jnp.exp(logits - highest)
    return scaled / jnp.sum(scaled, axis=-1, keepdims=True)


def project_pair(
    pair_block, mask_block, length, norm_gain, w_query, w_key, w_value, w_gate, head_count
):
    rows_n, cols_n, channels = pair_block.shape
    normed = (
        layer_norm(pair_block, norm_gain).astype(jnp.bfloat16).reshape(rows_n * cols_n, channels)
    )
    mask_cells = mask_block.astype(jnp.float32)[:, :, None]
    head_size = channels // head_count

    def linear(weight):
        return jnp.dot(normed, weight, preferred_element_type=jnp.float32).reshape(
            rows_n, cols_n, channels
        )

    query_rows = (linear(w_query) * mask_cells * (1.0 / math.sqrt(head_size))).astype(jnp.bfloat16)
    key_rows = (linear(w_key) * mask_cells * (1.0 / math.sqrt(length))).astype(jnp.bfloat16)
    value_rows = linear(w_value).astype(jnp.bfloat16)
    gate_values = jax.nn.sigmoid(linear(w_gate))
    return (query_rows, key_rows, value_rows, gate_values)


def finish_pass(pair_block, gate_values, mixed_heads, w_out):
    rows_n, cols_n, channels = pair_block.shape
    gated_rows = (gate_values * mixed_heads.reshape(rows_n, cols_n, channels)).astype(jnp.bfloat16)
    update = jnp.dot(
        gated_rows.reshape(rows_n * cols_n, channels), w_out, preferred_element_type=jnp.float32
    )
    return (pair_block.astype(jnp.float32) + update.reshape(rows_n, cols_n, channels)).astype(
        jnp.bfloat16
    )


def node_features(node_state, atom_type, type_table):
    onehot = (
        atom_type[:, None] == jnp.arange(type_table.shape[0], dtype=jnp.int32)[None, :]
    ).astype(jnp.float32)
    return node_state + jnp.dot(onehot, type_table, precision=PRECISE)


def edge_projection(pair_rows, spacing, edge_pair, edge_radial):
    rows_n, neighbour_count, channels = pair_rows.shape
    from_pair = jnp.dot(
        pair_rows.reshape(rows_n * neighbour_count, channels),
        edge_pair,
        preferred_element_type=jnp.float32,
    )
    basis = radial(spacing, edge_radial.shape[0]).reshape(
        rows_n * neighbour_count, edge_radial.shape[0]
    )
    from_radial = jnp.dot(basis, edge_radial, precision=PRECISE)
    return (from_pair + from_radial).reshape(rows_n, neighbour_count, edge_pair.shape[1])


def merge_parts(earlier_parts, later_parts):
    top_early, total_early, value_early, shift_early = earlier_parts
    top_late, total_late, value_late, shift_late = later_parts
    highest = jnp.maximum(top_early, top_late)
    scale_early = jnp.exp(top_early - highest)
    scale_late = jnp.exp(top_late - highest)
    return (
        highest,
        total_early * scale_early + total_late * scale_late,
        value_early * scale_early[:, :, None] + value_late * scale_late[:, :, None],
        shift_early * scale_early[None] + shift_late * scale_late[None],
    )


def row_pass(
    pair_block,
    mask_block,
    all_xyz,
    col_xyz,
    length,
    norm_gain,
    w_query,
    w_key,
    w_value,
    w_gate,
    w_out,
    w_bias,
):
    rows_n, cols_n, channels = pair_block.shape
    head_count = w_bias.shape[1]
    head_size = channels // head_count
    query_rows, key_rows, value_rows, gate_values = project_pair(
        pair_block, mask_block, length, norm_gain, w_query, w_key, w_value, w_gate, head_count
    )
    query_heads = query_rows.reshape(rows_n, cols_n, head_count, head_size)
    key_piece = lax.all_gather(key_rows, "col", axis=1, tiled=True)
    piece_cols = key_piece.shape[1]
    partial_value = jnp.einsum(
        "njhd,nkhd->hjk",
        query_heads,
        key_piece.reshape(rows_n, piece_cols, head_count, head_size),
        preferred_element_type=jnp.float32,
    )
    summed = lax.psum(partial_value, "row")
    weights = softmax_last(summed + pair_bias(col_xyz, all_xyz, w_bias)).astype(jnp.bfloat16)
    value_piece = lax.all_gather(value_rows, "col", axis=1, tiled=True)
    piece_cols = value_piece.shape[1]
    mixed_heads = jnp.einsum(
        "hjk,nkhd->njhd",
        weights,
        value_piece.reshape(rows_n, piece_cols, head_count, head_size),
        preferred_element_type=jnp.float32,
    )
    return finish_pass(pair_block, gate_values, mixed_heads, w_out)


def column_pass(
    pair_block,
    mask_block,
    all_xyz,
    row_xyz,
    length,
    norm_gain,
    w_query,
    w_key,
    w_value,
    w_gate,
    w_out,
    w_bias,
):
    rows_n, cols_n, channels = pair_block.shape
    head_count = w_bias.shape[1]
    head_size = channels // head_count
    query_rows, key_rows, value_rows, gate_values = project_pair(
        pair_block, mask_block, length, norm_gain, w_query, w_key, w_value, w_gate, head_count
    )
    query_heads = query_rows.reshape(rows_n, cols_n, head_count, head_size)
    key_piece = lax.all_gather(key_rows, "row", axis=0, tiled=True)
    piece_rows = key_piece.shape[0]
    partial_value = jnp.einsum(
        "inhd,mnhd->him",
        query_heads,
        key_piece.reshape(piece_rows, cols_n, head_count, head_size),
        preferred_element_type=jnp.float32,
    )
    summed = lax.psum(partial_value, "col")
    weights = softmax_last(summed + pair_bias(row_xyz, all_xyz, w_bias)).astype(jnp.bfloat16)
    value_piece = lax.all_gather(value_rows, "row", axis=0, tiled=True)
    piece_rows = value_piece.shape[0]
    mixed_heads = jnp.einsum(
        "him,mnhd->inhd",
        weights,
        value_piece.reshape(piece_rows, cols_n, head_count, head_size),
        preferred_element_type=jnp.float32,
    )
    return finish_pass(pair_block, gate_values, mixed_heads, w_out)


def shards(
    pair,
    pair_mask,
    node_state,
    coords,
    neighbours,
    atom_type,
    type_table,
    node_query,
    node_key,
    node_value,
    edge_pair,
    edge_radial,
    node_out_w,
    coord_gain,
    radial_pair,
    row_gain,
    row_query,
    row_key,
    row_value,
    row_gate,
    row_out,
    row_bias,
    column_gain,
    column_query,
    column_key,
    column_value,
    column_gate,
    column_out,
    column_bias,
):
    rows_n, cols_n, channels = pair.shape
    length = rows_n * lax.axis_size("row")
    node_width = node_state.shape[1]
    head_count = coord_gain.shape[0]
    head_size = node_width // head_count
    neighbour_count = neighbours.shape[1]
    row_start = lax.axis_index("row") * rows_n
    col_start = lax.axis_index("col") * cols_n
    features = node_features(node_state, atom_type, type_table)
    all_features, all_coords = (
        lax.all_gather(features, "row", axis=0, tiled=True),
        lax.all_gather(coords, "row", axis=1, tiled=True),
    )
    block_features = lax.dynamic_slice_in_dim(all_features, col_start, cols_n, 0)
    block_keys = jnp.dot(block_features, node_key, precision=PRECISE)
    block_values = jnp.dot(block_features, node_value, precision=PRECISE)
    query_rows = jnp.dot(features, node_query, precision=PRECISE).reshape(
        rows_n, head_count, head_size
    )
    owner_flag = neighbours // cols_n == lax.axis_index("col")
    local_index = jnp.clip(neighbours - col_start, 0, cols_n - 1)
    pair_rows = pair[jnp.arange(rows_n)[:, None], local_index]
    offsets = all_coords[:, neighbours] - coords[:, :, None]
    spacing = jnp.sqrt(jnp.sum(offsets * offsets, axis=0) + 1e-06)
    edge_terms = edge_projection(pair_rows, spacing, edge_pair, edge_radial)
    shaped = (rows_n, neighbour_count, head_count, head_size)
    key_rows = (block_keys[local_index] + edge_terms[:, :, :node_width]).reshape(shaped)
    value_rows = (block_values[local_index] + edge_terms[:, :, node_width:]).reshape(shaped)
    scores = jnp.sum(query_rows[:, None] * key_rows, axis=-1) * (1.0 / math.sqrt(head_size))
    owner_cells = owner_flag[:, :, None]
    masked = jnp.where(owner_cells, scores, NEGATIVE)
    highest = jnp.max(masked, axis=1)
    scaled = jnp.where(owner_cells, jnp.exp(masked - highest[:, None]), 0.0)
    weight_total = jnp.sum(scaled, axis=1)
    weighted = jnp.einsum("nkh,nkhd->nhd", scaled, value_rows, precision=PRECISE)
    shift_sum = jnp.einsum("nkh,cnk->cnh", scaled, offsets, precision=PRECISE)
    highest, weight_total, weighted, shift_sum = combined_all(
        (highest, weight_total, weighted, shift_sum), "col", merge_parts
    )
    attended = (weighted / weight_total[:, :, None]).reshape(rows_n, node_width)
    new_state = features + jnp.dot(attended, node_out_w, precision=PRECISE)
    new_coords = coords + jnp.sum(
        coord_gain[None, None, :] * shift_sum / weight_total[None], axis=2
    )
    all_xyz = lax.all_gather(new_coords, "row", axis=1, tiled=True)
    row_xyz = lax.dynamic_slice_in_dim(all_xyz, row_start, rows_n, 1)
    col_xyz = lax.dynamic_slice_in_dim(all_xyz, col_start, cols_n, 1)
    basis = radial(distances(row_xyz, col_xyz), radial_pair.shape[0])
    added = jnp.dot(
        basis.reshape(rows_n * cols_n, radial_pair.shape[0]), radial_pair, precision=PRECISE
    )
    pair_rbf = (pair.astype(jnp.float32) + added.reshape(rows_n, cols_n, channels)).astype(
        jnp.bfloat16
    )
    after_rows = row_pass(
        pair_rbf,
        pair_mask,
        all_xyz,
        col_xyz,
        length,
        row_gain,
        row_query,
        row_key,
        row_value,
        row_gate,
        row_out,
        row_bias,
    )
    pair_out = column_pass(
        after_rows,
        pair_mask,
        all_xyz,
        row_xyz,
        length,
        column_gain,
        column_query,
        column_key,
        column_value,
        column_gate,
        column_out,
        column_bias,
    )
    return (pair_out, new_state, new_coords)


def solution(mesh):
    placed = (
        P("row", "col", None),
        P("row", "col"),
        P("row", None),
        P(None, "row"),
        P("row", None),
        P("row"),
        P(),
        P(),
        P(),
        P(),
        P(),
        P(),
        P(),
        P(),
        P(),
        P(),
        P(),
        P(),
        P(),
        P(),
        P(),
        P(),
        P(),
        P(),
        P(),
        P(),
        P(),
        P(),
        P(),
    )
    return jax.shard_map(
        shards,
        mesh=mesh,
        in_specs=placed,
        out_specs=(P("row", "col", None), P("row", None), P(None, "row")),
        check_vma=False,
    )
```

profile of v0, /device:TPU:0, one launch (start us, length us, event | category | flops | bytes accessed | tf_op | source)
XLA Modules:
  0.0 662.9 jit_solution(874421756151965643)
XLA Ops:
  10.5 24.3 %all_gather.45 = f32[640,64]{1,0:T(8,128)S(1)} all-gather(f32[40,64]{1,0:T(8,128)S(1)} %convolution_add_fusion.1), channel_id=1, replica_groups=mesh['row'=16,'col'=8] {'row'}, dimensions={0}, use_global_device_ids=true | all-gather | bytes 174080 | tf_op jit(solution)/shard_map/all_gather | solution.py:253
  42.2 22.8 %all-gather.4 = f32[16,40,3]{1,2,0:T(4,128)S(1)} all-gather(f32[1,40,3]{1,2,0:T(4,128)S(1)} %bitcast.221), channel_id=1, replica_groups=mesh['row'=16,'col'=8] {'row'}, dimensions={0}, use_global_device_ids=true | all-gather | bytes 8160 | tf_op jit(solution)/shard_map/all_gather | solution.py:254
  70.6 13.8 %gather_fusion.1 = bf16[2560,128]{1,0:T(8,128)(2,1)S(1)} fusion(bf16[40,80,128]{2,1,0:T(8,128)(2,1)S(1)} %copy-done.2, s32[2560]{0:T(1024)S(1)} %reshape.216), kind=kCustom, calls=%fused_computation.1 | custom fusion | bytes 1331200 | tf_op jit(solution)/shard_map/gather | solution.py:264
  109.6 14.6 %all-gather.2 = f32[320,4,16]{2,1,0:T(4,128)S(1)} all-gather(f32[40,4,16]{2,1,0:T(4,128)S(1)} %bitcast.213), channel_id=4, replica_groups=mesh['row'=16,'col'=8] {'col'}, dimensions={0}, use_global_device_ids=true | all-gather | bytes 92160 | tf_op jit(solution)/shard_map/all_gather | solution.py:14
  124.6 12.8 %all-gather.3 = f32[24,40,4]{1,2,0:T(4,128)S(1)} all-gather(f32[3,40,4]{1,2,0:T(4,128)S(1)} %copy.166), channel_id=5, replica_groups=mesh['row'=16,'col'=8] {'col'}, dimensions={0}, use_global_device_ids=true | all-gather | bytes 17280 | tf_op jit(solution)/shard_map/all_gather | solution.py:14
  137.5 11.2 %all-gather.6 = f32[8,40,4]{1,2,0:T(4,128)S(1)} all-gather(f32[1,40,4]{1,2,0:T(4,128)S(1)} %copy.162), channel_id=3, replica_groups=mesh['row'=16,'col'=8] {'col'}, dimensions={0}, use_global_device_ids=true | all-gather | bytes 5760 | tf_op jit(solution)/shard_map/all_gather | solution.py:14
  148.8 11.3 %all-gather.5 = f32[8,40,4]{1,2,0:T(4,128)S(1)} all-gather(f32[1,40,4]{1,2,0:T(4,128)S(1)} %copy.161), channel_id=2, replica_groups=mesh['row'=16,'col'=8] {'col'}, dimensions={0}, use_global_device_ids=true | all-gather | bytes 5760 | tf_op jit(solution)/shard_map/all_gather | solution.py:14
  161.4 21.2 %all-gather.7 = f32[16,40,3]{1,2,0:T(4,128)S(1)} all-gather(f32[1,40,3]{1,2,0:T(4,128)S(1)} %bitcast.222), channel_id=1, replica_groups=mesh['row'=16,'col'=8] {'row'}, dimensions={0}, use_global_device_ids=true | all-gather | bytes 8160 | tf_op jit(solution)/shard_map/all_gather | solution.py:287
  197.0 34.3 %all-gather.15.cloned.1.call-done = bf16[40,640,128]{2,1,0:T(8,128)(2,1)} async-done(((bf16[40,80,128]{2,1,0:T(8,128)(2,1)}), bf16[40,640,128]{2,1,0:T(8,128)(2,1)}) %all-gather.15.cloned.1.call-update) | async-done | bytes 6553616 | tf_op jit(solution)/shard_map/all_gather | solution.py:149
  231.3 9.5 %copy.173 = bf16[40,640,128]{1,2,0:T(8,128)(2,1)} copy(bf16[40,640,128]{2,1,0:T(8,128)(2,1)} %all-gather.15.cloned.1.call-done) | data formatting | bytes 13107200 | tf_op jit(solution)/shard_map/all_gather | solution.py:149
  246.6 10.8 %while.42 = (s32[]{:T(128)}, f32[5,4,80,128]{3,1,2,0:T(4,128)S(1)}, f32[3,80]{1,0:T(4,128)S(1)}, f32[5,3,128]{2,1,0:T(4,128)S(1)}, f32[64,4]{0,1:T(4,128)S(1)}, /*index=5*/s32[]{:T(128)}) while((s32[]{:T(128)}, f32[5,4,80,128]{3,1,2,0:T(4,128)S(1)}, f32[3,80]{1,0:T(4,128)S(1)}, f32[5,3,128]{2,1,0:T(4,128)S(1)}, f32[64,4]{0,1:T(4,128)S(1)}, ...), condition=%wide.region_13.14_spmd, body=%wide.region_11.13_spmd.sunk | while | flops 34170944 | bytes 336141 | solution.py:43
  258.1 17.7 %all-gather.13.cloned.1.call-done = bf16[40,640,128]{2,1,0:T(8,128)(2,1)} async-done(((bf16[40,80,128]{2,1,0:T(8,128)(2,1)}), bf16[40,640,128]{2,1,0:T(8,128)(2,1)}) %all-gather.13.cloned.1.call-update) | async-done | bytes 6553616 | tf_op jit(solution)/shard_map/all_gather | solution.py:159
  275.8 9.5 %copy.171 = bf16[40,640,128]{1,2,0:T(8,128)(2,1)} copy(bf16[40,640,128]{2,1,0:T(8,128)(2,1)} %all-gather.13.cloned.1.call-done) | data formatting | bytes 13107200 | tf_op jit(solution)/shard_map/all_gather | solution.py:159
  285.3 79.3 %all-reduce.3.cloned.1.call-done = f32[4,80,640]{2,1,0:T(8,128)} async-done(((f32[4,80,640]{2,1,0:T(8,128)}), f32[4,80,640]{2,1,0:T(8,128)}) %all-reduce.3.cloned.1.call-update) | async-done | bytes 819216 | tf_op jit(solution)/shard_map/psum | solution.py:157
  366.1 6.5 fusion.53
  386.5 6.2 while.43
  396.6 5.7 copy.182
  402.2 73.6 %all-gather.19.cloned.1.call-done = bf16[640,80,128]{2,1,0:T(8,128)(2,1)} async-done(((bf16[40,80,128]{2,1,0:T(8,128)(2,1)}), bf16[640,80,128]{2,1,0:T(8,128)(2,1)}) %all-gather.19.cloned.1.call-update) | async-done | bytes 13107216 | tf_op jit(solution)/shard_map/all_gather | solution.py:191
  475.8 21.1 %copy.181 = bf16[640,80,128]{0,2,1:T(8,128)(2,1)} copy(bf16[640,80,128]{2,1,0:T(8,128)(2,1)} %all-gather.19.cloned.1.call-done) | data formatting | bytes 26214400 | tf_op jit(solution)/shard_map/all_gather | solution.py:191
  496.9 7.7 %fusion.77 = f32[4,40,640]{2,1,0:T(8,128)} fusion(bf16[40,80,4,32]{0,3,1,2:T(8,128)(2,1)S(1)} %copy.182, bf16[640,80,4,32]{0,3,2,1:T(8,128)(2,1)} %bitcast.195), kind=kOutput, calls=%fused_computation.101 | convolution fusion | flops 524288000 | bytes 14336000 | tf_op jit(solution)/shard_map/inhd,mnhd->him/dot_general | solution.py:193
  505.5 64.5 %all-gather.17.cloned.1.call-done = bf16[640,80,128]{2,1,0:T(8,128)(2,1)} async-done(((bf16[40,80,128]{2,1,0:T(8,128)(2,1)}), bf16[640,80,128]{2,1,0:T(8,128)(2,1)}) %all-gather.17.cloned.1.call-update) | async-done | bytes 13107216 | tf_op jit(solution)/shard_map/all_gather | solution.py:201
  570.0 21.1 %copy.179 = bf16[640,80,128]{0,2,1:T(8,128)(2,1)} copy(bf16[640,80,128]{2,1,0:T(8,128)(2,1)} %all-gather.17.cloned.1.call-done) | data formatting | bytes 26214400 | tf_op jit(solution)/shard_map/all_gather | solution.py:201
  591.1 41.6 %all-reduce.5.cloned.1.call-done = f32[4,40,640]{2,1,0:T(8,128)} async-done(((f32[4,40,640]{2,1,0:T(8,128)}), f32[4,40,640]{2,1,0:T(8,128)}) %all-reduce.5.cloned.1.call-update) | async-done | bytes 409616 | tf_op jit(solution)/shard_map/psum | solution.py:199
  634.0 10.7 %fusion.46 = f32[40,80,4,32]{0,3,1,2:T(8,128)} fusion(bf16[640,80,4,32]{0,3,2,1:T(8,128)(2,1)} %bitcast.197, f32[4,40,640]{2,1,0:T(8,128)S(1)} %get-tuple-element.412, f32[4,40]{1,0:T(4,128)S(1)} %get-tuple-element.411), kind=kOutput, calls=%fused_computation.63 | convolution fusion | flops 524492800 | bytes 15155840 | tf_op jit(solution)/shard_map/him,mnhd->inhd/dot_general | solution.py:203
  (252 shorter events, 112.7 us)
Async XLA Ops:
  7.2 175.9 %copy-start = (f32[64,128]{1,0:T(8,128)S(1)}, f32[64,128]{1,0:T(8,128)}, u32[]{:S(2)}) copy-start(f32[64,128]{1,0:T(8,128)} %param.49) | copy-start | bytes 98308
  7.2 224.1 %all-gather.15.cloned.1.call-start = ((), (), s32[]{:S(2)}) async-start(), calls=%async_computation.1 | async-start | bytes 7372800 | tf_op jit(solution)/shard_map/all_gather | solution.py:149
  7.2 77.5 %copy-start.23 = (f32[64]{0:T(128)}, f32[64]{0:T(128)S(1)}, u32[]{:S(2)}) copy-start(f32[64]{0:T(128)S(1)} %iota_multiply_fusion.2) | copy-start | bytes 772
  42.1 28.5 %copy-start.2 = (bf16[40,80,128]{2,1,0:T(8,128)(2,1)S(1)}, bf16[40,80,128]{2,1,0:T(8,128)(2,1)}, u32[]{:S(2)}) copy-start(bf16[40,80,128]{2,1,0:T(8,128)(2,1)} %param.35) | copy-start | bytes 2457604
  42.2 42.2 %copy-start.13 = (f32[3,40]{0,1:T(8,128)}, f32[3,40]{0,1:T(8,128)S(1)}, u32[]{:S(2)}) copy-start(f32[3,40]{0,1:T(8,128)S(1)} %copy.158) | copy-start | bytes 1444
  70.6 13.8 %copy-start.15 = (bf16[128,128]{1,0:T(8,128)(2,1)S(1)}, bf16[128,128]{1,0:T(8,128)(2,1)}, u32[]{:S(2)}) copy-start(bf16[128,128]{1,0:T(8,128)(2,1)} %param.45) | copy-start | bytes 98308
  88.5 5.5 copy-start.17
  107.4 17.2 %copy-start.12 = (f32[3,40,4]{2,0,1:T(4,128)S(1)}, f32[3,40,4]{2,0,1:T(4,128)}, u32[]{:S(2)}) copy-start(f32[3,40,4]{2,0,1:T(4,128)} %convolution_bitcast_fusion.1) | copy-start | bytes 5764
  107.4 30.1 %copy-start.11 = (f32[40,4]{1,0:T(8,128)S(1)}, f32[40,4]{1,0:T(8,128)}, u32[]{:S(2)}) copy-start(f32[40,4]{1,0:T(8,128)} %get-tuple-element.401) | copy-start | bytes 1924
  107.4 41.4 %copy-start.10 = (f32[40,4]{1,0:T(8,128)S(1)}, f32[40,4]{1,0:T(8,128)}, u32[]{:S(2)}) copy-start(f32[40,4]{1,0:T(8,128)} %copy-done.9) | copy-start | bytes 1924
  109.6 51.2 %copy-start.25 = (f32[4]{0:T(128)S(1)}, f32[4]{0:T(128)}, u32[]{:S(2)}) copy-start(f32[4]{0:T(128)} %param.48) | copy-start | bytes 52
  109.6 51.2 %copy-start.21 = (f32[3,40]{1,0:T(4,128)S(1)}, f32[3,40]{1,0:T(4,128)}, u32[]{:S(2)}) copy-start(f32[3,40]{1,0:T(4,128)} %param.38) | copy-start | bytes 1444
  109.6 73.4 %copy-start.24 = (f32[64]{0:T(128)S(1)}, f32[64]{0:T(128)}, u32[]{:S(2)}) copy-start(f32[64]{0:T(128)} %copy-done.23) | copy-start | bytes 772
  186.5 6.1 copy-start.5
  190.5 85.3 %all-gather.13.cloned.1.call-start = ((), (), s32[]{:S(2)}) async-start(), calls=%async_computation | async-start | bytes 7372800 | tf_op jit(solution)/shard_map/all_gather | solution.py:159
  192.6 172.0 %all-reduce.3.cloned.1.call-start = ((), (), s32[]{:S(2)}) async-start(), calls=%async_computation.2 | async-start | bytes 1638400 | tf_op jit(solution)/shard_map/psum | solution.py:157
  240.8 5.8 copy-start.35
  246.3 229.5 %all-gather.19.cloned.1.call-start = ((), (), s32[]{:S(2)}) async-start(), calls=%async_computation.4 | async-start | bytes 13926400 | tf_op jit(solution)/shard_map/all_gather | solution.py:191
  376.6 4.8 copy-start.31
  376.6 4.8 copy-start.38
  380.1 13.0 %copy-start.3 = (bf16[40,80,128]{2,1,0:T(8,128)(2,1)}, bf16[40,80,128]{2,1,0:T(8,128)(2,1)S(1)}, u32[]{:S(2)}) copy-start(bf16[40,80,128]{2,1,0:T(8,128)(2,1)S(1)} %get-tuple-element.410) | copy-start | bytes 2457604
  384.1 186.0 %all-gather.17.cloned.1.call-start = ((), (), s32[]{:S(2)}) async-start(), calls=%async_computation.3 | async-start | bytes 13926400 | tf_op jit(solution)/shard_map/all_gather | solution.py:201
  386.2 246.6 %all-reduce.5.cloned.1.call-start = ((), (), s32[]{:S(2)}) async-start(), calls=%async_computation.5 | async-start | bytes 819200 | tf_op jit(solution)/shard_map/psum | solution.py:199
  496.9 7.8 %copy-start.18 = (f32[64,64]{1,0:T(8,128)S(1)}, f32[64,64]{1,0:T(8,128)}, u32[]{:S(2)}) copy-start(f32[64,64]{1,0:T(8,128)} %param.47) | copy-start | bytes 49156
  (22 other events, 46.2 us)
Sparse Core Ops, SparseCore 0:
  190.6 40.6 all-gather.14
  233.6 42.1 all-gather.12
  279.1 85.4 all-reduce.2
  384.2 91.5 all-gather.18
  477.8 92.1 all-gather.16
  572.2 60.4 all-reduce.4
where the time goes:
time: 674 us; the launch traced here: 663 us
  waiting for transfers between devices  311 us (46%)
  local copies, waits for them, and re-layouts  122 us (18%)
  blocking collectives  118 us (18%)
  matrix products  80.3 us (12%)
  between operations  15.3 us (2%)
  other arithmetic  14.5 us (2%)
    psum x1, waiting for transfers between devices, row_pass(): summed = lax.psum(partial_value, 'row')  79.3 us
    all_gather x1, waiting for transfers between devices, column_pass(): key_piece = lax.all_gather(key_rows, 'row', axis=0, tiled=True)  73.6 us
    all_gather x1, waiting for transfers between devices, column_pass(): value_piece = lax.all_gather(value_rows, 'row', axis=0, tiled=True)  64.5 us
    all_gather x4, blocking collectives, combined_all(): everything = jax.tree.map(lambda part: lax.all_gather(part, axis), x)  49.9 us
    psum x1, waiting for transfers between devices, column_pass(): summed = lax.psum(partial_value, 'col')  41.6 us
    all_gather x1, waiting for transfers between devices, row_pass(): key_piece = lax.all_gather(key_rows, 'col', axis=1, tiled=True)  34.3 us
    all_gather x1, blocking collectives, shards(): lax.all_gather(features, 'row', axis=0, tiled=True)  24.3 us
    all_gather x1, blocking collectives, shards(): lax.all_gather(coords, 'row', axis=1, tiled=True)  22.8 us
  transfers between devices with their start and end apart: 6, of which 6 were waited for; matrix products, arithmetic and copies ran while one was open for 17% of the time, Pallas kernels for 0%

commit v1 on v0

v1 whole, which is shorter than its diff:
```python
import functools
import math

import jax
import jax.numpy as jnp
from jax import lax
from jax.experimental import pallas as pl
from jax.experimental.pallas import tpu as pltpu
from jax.sharding import Mesh
from jax.sharding import PartitionSpec as P

BF16 = jnp.bfloat16
F32 = jnp.float32
PRECISE = lax.Precision.HIGHEST
RADIAL_REACH = 24.0
NEGATIVE = -1e30
EVERYWHERE = ("x", "y", "z", "core")

VMEM = pl.BlockSpec(memory_space=pltpu.VMEM)
SMEM = pl.BlockSpec(memory_space=pltpu.SMEM)
PARAMS = pltpu.CompilerParams(vmem_limit_bytes=44 * 1024 * 1024)

ROWS, COLS, CH, HEADS = 40, 80, 128, 4
LENGTH = 640
LANES = 128
SLOT = 32
BLOCK = 32
OWNERS = 10
HALF = LENGTH // 2


def call(kernel, out_shape, in_specs, scratch=(), cost=None, out_specs=None):
    if out_specs is None:
        out_specs = jax.tree.map(lambda _: VMEM, out_shape)
    return pl.pallas_call(
        kernel,
        out_shape=out_shape,
        in_specs=in_specs,
        out_specs=out_specs,
        scratch_shapes=list(scratch),
        compiler_params=PARAMS,
        cost_estimate=cost,
    )


def shape(dims, dtype):
    return jax.ShapeDtypeStruct(dims, dtype)


def iota(dims, axis):
    return lax.broadcasted_iota(jnp.int32, dims, axis)


def dot(a, b):
    return jnp.dot(a, b, preferred_element_type=F32)


def dot32(a, b):
    return jnp.dot(a, b, preferred_element_type=F32, precision=PRECISE)


def split(a):
    high = a.astype(BF16)
    return high, (a - high.astype(F32)).astype(BF16)


def graph_kernel(
    start_ref, xyz_ref, pair_ref, near_ref, far_ref, neigh_ref, wq_ref, wkv_ref, ep_ref, er_ref,
    out_ref, q_ref,
):
    step = 8
    bins = 64
    far = far_ref[...]
    q_ref[...] = dot32(near_ref[...], wq_ref[...])
    base = dot32(far, wkv_ref[...])
    far_xyz = [jnp.broadcast_to(far[:, 64 + c : 65 + c], (COLS, LANES)) for c in range(3)]
    lane = iota((1, LANES), 1)
    centers = (lane % bins).astype(F32) * (RADIAL_REACH / (bins - 1))
    width = bins / RADIAL_REACH
    of_lane, to_lane = iota((LANES, LANES), 0), iota((LANES, LANES), 1)
    head_sum = jnp.where((of_lane < 64) & (of_lane // 16 == (to_lane % 64) // 16), 1.0, 0.0)
    ones = jnp.ones((64, LANES), BF16)
    cell = iota((COLS, 64), 0) + start_ref[0]
    slot = lane % 16

    def some(block, carry):
        first = pl.multiple_of(block * step, step)
        offsets, bases, counts, queries = [], [], [], []
        neigh = neigh_ref[pl.ds(first, step), :]
        q_some = q_ref[pl.ds(first, step), :]
        for u in range(step):
            off = [far_xyz[c] - xyz_ref[c, first + u] for c in range(3)]
            spacing = jnp.sqrt(off[0] * off[0] + off[1] * off[1] + off[2] * off[2] + 1e-06)
            away = (spacing - centers) * width
            bases.append(jnp.exp(-(away * away)))
            offsets.append(off)
            counts.append(jnp.where(cell == neigh[u : u + 1, :], 1.0, 0.0).astype(BF16))
            queries.append(q_some[u : u + 1, :])
        cells = pair_ref[pl.ds(first, step)].reshape(step * COLS, CH)
        edge = dot(cells, ep_ref[...]) + dot32(jnp.concatenate(bases, 0), er_ref[...])
        count = dot(jnp.concatenate(counts, 0), ones)
        edges, products = [], []
        for u in range(step):
            one = edge[u * COLS : (u + 1) * COLS] + base
            edges.append(one)
            products.append(one * queries[u])
        scores = dot32(jnp.concatenate(products, 0), head_sum)
        lines = []
        for u in range(step):
            times = count[u * COLS : (u + 1) * COLS]
            score = jnp.where(times > 0.0, scores[u * COLS : (u + 1) * COLS], NEGATIVE)
            top = jnp.max(score, axis=0, keepdims=True)
            w = times * jnp.exp(score - top)
            total = jnp.sum(w, axis=0, keepdims=True)
            shift = [jnp.sum(w * offsets[u][c], axis=0, keepdims=True) for c in range(3)]
            value = jnp.sum(w * edges[u], axis=0, keepdims=True)
            small = jnp.where(slot == 0, top, 0.0)
            for at, entry in enumerate([total] + shift):
                small = jnp.where(slot == at + 1, entry, small)
            lines.append(jnp.where(lane < 64, small, value))
        out_ref[pl.ds(first, step), :] = jnp.concatenate(lines, 0)
        return carry

    lax.fori_loop(0, ROWS // step, some, 0)


def merge_kernel(gain_ref, parts_ref, near_ref, wo_ref, out_ref):
    of_lane, to_lane = iota((LANES, LANES), 0), iota((LANES, LANES), 1)
    home = ((to_lane % 64) // 16) * 16
    to_top = jnp.where(of_lane == home, 1.0, 0.0)
    to_total = jnp.where(of_lane == home + 1, 1.0, 0.0)
    gain = jnp.zeros((LANES, LANES), F32)
    for head in range(4):
        for c in range(3):
            at = (of_lane == head * 16 + 2 + c) & (to_lane == 64 + c)
            gain = jnp.where(at, gain_ref[head], gain)
    count = parts_ref.shape[0]
    parts = [parts_ref[p] for p in range(count)]
    tops = [dot32(part, to_top) for part in parts]
    highest = functools.reduce(jnp.maximum, tops)
    merged = sum(jnp.exp(top - highest) * part for top, part in zip(tops, parts))
    ratio = merged / dot32(merged, to_total)
    out_ref[...] = near_ref[...] + dot32(ratio, wo_ref[...] + gain)


def widen(weight_ref, wide_ref, column):
    weight = weight_ref[...].astype(F32)
    lane = iota((CH, LANES), 1)
    for h in range(HEADS):
        for i in range(4):
            turned = pltpu.roll(weight, ((i - h) * SLOT) % LANES, 1) if i != h else weight
            wide_ref[i * CH : (i + 1) * CH, column + h * LANES : column + (h + 1) * LANES] = (
                jnp.where(lane // SLOT == i, turned, 0.0).astype(BF16)
            )


def widen_out(weight_ref, wide_ref):
    wide_ref[...] = jnp.zeros_like(wide_ref)
    for h in range(HEADS):
        for i in range(4):
            wide_ref[
                h * LANES + i * SLOT : h * LANES + (i + 1) * SLOT, i * CH : (i + 1) * CH
            ] = weight_ref[h * SLOT : (h + 1) * SLOT, :]


def normed(rounded, norm_gain):
    mean_of = jnp.full((CH, LANES), 1.0 / CH, BF16)
    centered = rounded.astype(F32) - dot(rounded, mean_of)
    high, low = split(centered * centered)
    spread = dot(high, mean_of) + dot(low, mean_of)
    return centered * lax.rsqrt(spread + 1e-05) * norm_gain


def spread_mask(mask, group):
    n = mask.shape[1]
    pick = iota((n, LANES), 0) == 4 * group + iota((n, LANES), 1) // SLOT
    return dot(mask, jnp.where(pick, 1.0, 0.0).astype(BF16))


def put_projections(z, mask, wide_ref, put):
    scales = (1.0 / math.sqrt(SLOT), 1.0 / math.sqrt(LENGTH))
    for matrix in range(4):
        wide = HEADS * LANES
        out = dot(z, wide_ref[:, matrix * wide : (matrix + 1) * wide])
        for h in range(HEADS):
            one = out[:, h * LANES : (h + 1) * LANES]
            if matrix < 2:
                one = one * mask * scales[matrix]
            put(matrix, h, one)


def row_start_kernel(
    xyz_ref, pair_ref, far_ref, mask_ref, radial_ref, gain_ref, wq_ref, wk_ref, wv_ref, wg_ref,
    x_ref, qkv_ref, gate_ref, z_ref, wide_ref,
):
    bins = 64
    for at, ref in enumerate((wq_ref, wk_ref, wv_ref, wg_ref)):
        widen(ref, wide_ref, at * HEADS * LANES)
    far = far_ref[...]
    far_xyz = [jnp.broadcast_to(far[:, 64 + c : 65 + c], (COLS, LANES)) for c in range(3)]
    lane = iota((1, LANES), 1)
    centers = (lane % bins).astype(F32) * (RADIAL_REACH / (bins - 1))
    width = bins / RADIAL_REACH
    table = radial_ref[...]
    blank = jnp.zeros_like(table)
    table = jnp.concatenate(
        [jnp.concatenate([table, blank], 1), jnp.concatenate([blank, table], 1)], 0
    )
    table_high, table_low = split(table)
    table = jnp.concatenate([table_high, table_low, table_high], 0)
    norm_gain = gain_ref[...]

    def some(group, carry):
        bases = []
        for at in range(2):
            n = group * 4 + at * 2
            off = [
                far_xyz[c] - jnp.where(lane < bins, xyz_ref[c, n], xyz_ref[c, n + 1])
                for c in range(3)
            ]
            spacing = jnp.sqrt(off[0] * off[0] + off[1] * off[1] + off[2] * off[2] + 1e-06)
            away = (spacing - centers) * width
            bases.append(jnp.exp(-(away * away)))
        high, low = split(jnp.concatenate(bases, 0))
        added = dot(jnp.concatenate([high, high, low], 1), table)
        rows = []
        for i in range(4):
            at = (i // 2) * COLS
            part = added[at : at + COLS, (i % 2) * CH : (i % 2 + 1) * CH]
            rows.append((pair_ref[group * 4 + i].astype(F32) + part).astype(BF16))
            x_ref[group * 4 + i] = rows[-1]
        z = normed(jnp.concatenate(rows, 0), norm_gain).astype(BF16)
        for i in range(4):
            z_ref[pl.ds(pl.multiple_of(group * COLS, COLS), COLS), i * CH : (i + 1) * CH] = z[
                i * COLS : (i + 1) * COLS
            ]
        return carry

    groups = ROWS // 4
    lax.fori_loop(0, groups, some, 0)
    size = groups // 2 * COLS
    for s in range(2):
        mask = jnp.concatenate(
            [spread_mask(mask_ref[...], s * (groups // 2) + g) for g in range(groups // 2)], 0
        )

        def put(matrix, h, one):
            if matrix < 3:
                qkv_ref[h * 2 + s, matrix] = one.astype(BF16)
            else:
                gate_ref[h, s] = jax.nn.sigmoid(one)

        put_projections(z_ref[s * size : (s + 1) * size, :], mask, wide_ref, put)


def gathered(parts_ref, which, g, across):
    count = parts_ref.shape[0]
    if across == COLS:
        return jnp.concatenate(
            [parts_ref[p, which, g * across : (g + 1) * across, :] for p in range(count)], 0
        )
    return jnp.concatenate(
        [
            parts_ref[p, which].astype(F32)[g * across : (g + 1) * across]
            for p in range(count)
        ],
        0,
    ).astype(BF16)


def logits_kernel(across, core_ref, qkv_ref, own_ref, other_ref, q_ref, k_ref, sum_ref):
    for g in range(5):
        q_ref[:, g * LANES : (g + 1) * LANES] = gathered(qkv_ref, 0, g, across)
        k_ref[:, g * LANES : (g + 1) * LANES] = gathered(qkv_ref, 1, g, across)
    rows = 128
    for m in range(LENGTH // rows):
        sum_ref[m * rows : (m + 1) * rows, :] = lax.dot_general(
            q_ref[m * rows : (m + 1) * rows, :],
            k_ref[...],
            (((1,), (1,)), ((), ())),
            preferred_element_type=F32,
        )
    core = core_ref[0]
    own_ref[...] = sum_ref[pl.ds(pl.multiple_of(core * HALF, HALF), HALF), :]
    other_ref[...] = sum_ref[pl.ds(pl.multiple_of((1 - core) * HALF, HALF), HALF), :].astype(BF16)


def join_kernel(own_ref, other_ref, out_ref):
    out_ref[OWNERS:] = jnp.zeros((out_ref.shape[0] - OWNERS, BLOCK, LENGTH), BF16)
    for m in range(OWNERS):
        at = slice(m * BLOCK, (m + 1) * BLOCK)
        out_ref[m] = (own_ref[at, :] + other_ref[at, :].astype(F32)).astype(BF16)


def bias_kernel(weight_ref, near_ref, far_ref, out_ref):
    bins = 64
    near, far = near_ref[...], far_ref[...]
    square = jnp.zeros((BLOCK, LENGTH), F32)
    for c in range(3):
        off = near[:, c : c + 1] - far[c : c + 1, :]
        square = square + off * off
    width = bins / RADIAL_REACH
    spacing = jnp.sqrt(square + 1e-06) * width

    def some(at, total):
        for u in range(8):
            b = at * 8 + u
            away = spacing - b.astype(F32) * (width * RADIAL_REACH / (bins - 1))
            total = total + weight_ref[b] * jnp.exp(-(away * away))
        return total

    out_ref[...] = lax.fori_loop(0, bins // 8, some, jnp.zeros((BLOCK, LENGTH), F32))


def softmax_kernel(parts_ref, bias_ref, out_ref):
    count = parts_ref.shape[0]
    logits = bias_ref[...]
    for p in range(count):
        logits = logits + parts_ref[p].astype(F32)
    scaled = jnp.exp(logits - jnp.max(logits, axis=-1, keepdims=True))
    weights = (scaled / jnp.sum(scaled, axis=-1, keepdims=True)).astype(BF16)
    for p in range(count):
        out_ref[p] = weights


def mix_kernel(across, core_ref, own_ref, other_ref, qkv_ref, out_ref, a_ref, v_ref):
    core = core_ref[0]
    for m in range(OWNERS):
        at = pl.multiple_of(core * HALF + m * BLOCK, BLOCK)
        a_ref[pl.ds(at, BLOCK), :] = own_ref[m]
        at = pl.multiple_of((1 - core) * HALF + m * BLOCK, BLOCK)
        a_ref[pl.ds(at, BLOCK), :] = other_ref[m]
    for g in range(5):
        v_ref[:, g * LANES : (g + 1) * LANES] = gathered(qkv_ref, 2, g, across)
    rows = 160
    for m in range(LENGTH // rows):
        mixed = dot(a_ref[m * rows : (m + 1) * rows, :], v_ref[...])
        for p in range(rows // across):
            pieces = [
                mixed[p * across : (p + 1) * across, g * LANES : (g + 1) * LANES]
                for g in range(5)
            ]
            spare = out_ref.shape[1] - 5 * across
            if spare:
                pieces.append(jnp.zeros((spare, LANES), F32))
            out_ref[m * (rows // across) + p] = jnp.concatenate(pieces, 0).astype(BF16)


def column_start_kernel(
    x_ref, gate_ref, mixed_ref, mask_ref, wo_ref, gain_ref, wq_ref, wk_ref, wv_ref, wg_ref,
    new_ref, qkv_ref, next_gate_ref, z_ref, wide_out_ref, wide_ref,
):
    widen_out(wo_ref, wide_out_ref)
    for at, ref in enumerate((wq_ref, wk_ref, wv_ref, wg_ref)):
        widen(ref, wide_ref, at * HEADS * LANES)
    norm_gain = gain_ref[...]
    for s in range(2):
        gated = jnp.concatenate(
            [
                (gate_ref[h, s] * mixed_ref[h * 2 + s].astype(F32)).astype(BF16)
                for h in range(HEADS)
            ],
            1,
        )
        update = dot(gated, wide_out_ref[...])
        for g in range(5):
            rows = []
            for i in range(4):
                n = (s * 5 + g) * 4 + i
                part = update[g * COLS : (g + 1) * COLS, i * CH : (i + 1) * CH]
                rows.append((x_ref[n].astype(F32) + part).astype(BF16))
                new_ref[n] = rows[-1]
            z = normed(jnp.concatenate(rows, 0), norm_gain)
            first = (s * 5 + g) * 4 * COLS
            z_ref[first : first + 4 * COLS, :] = z
    for chunk in range(4):
        pieces, masks = [], []
        for g in range(5):
            column = (chunk * 5 + g) * 4
            pieces.append(
                jnp.concatenate(
                    [z_ref[pl.ds(column + i, ROWS, stride=COLS), :] for i in range(4)], 1
                )
            )
            masks.append(spread_mask(mask_ref[...], chunk * 5 + g))

        def put(matrix, h, one):
            if matrix < 3:
                spare = qkv_ref.shape[2] - one.shape[0]
                qkv_ref[h * 4 + chunk, matrix] = jnp.concatenate(
                    [one, jnp.zeros((spare, LANES), F32)], 0
                ).astype(BF16)
            else:
                next_gate_ref[h, chunk] = jax.nn.sigmoid(one)

        put_projections(
            jnp.concatenate(pieces, 0).astype(BF16), jnp.concatenate(masks, 0), wide_ref, put
        )


def finish_kernel(x_ref, gate_ref, mixed_ref, wo_ref, out_ref, turned_ref, wide_out_ref):
    widen_out(wo_ref, wide_out_ref)
    for chunk in range(4):
        gated = jnp.concatenate(
            [
                gate_ref[h, chunk] * mixed_ref[h * 4 + chunk].astype(F32)[: 5 * ROWS]
                for h in range(HEADS)
            ],
            1,
        ).astype(BF16)
        update = dot(gated, wide_out_ref[...])
        for g in range(5):
            for i in range(4):
                column = (chunk * 5 + g) * 4 + i
                turned_ref[pl.ds(column, ROWS, stride=COLS), :] = update[
                    g * ROWS : (g + 1) * ROWS, i * CH : (i + 1) * CH
                ]
    for n in range(ROWS):
        out_ref[n] = (x_ref[n].astype(F32) + turned_ref[n * COLS : (n + 1) * COLS, :]).astype(BF16)


def exchange(parts, axes):
    return lax.all_to_all(parts, axes, split_axis=0, concat_axis=0, tiled=True)


def swap_cores(x):
    return lax.ppermute(x, "core", [(0, 1), (1, 0)])


def column_tokens(mine, row, cols_n):
    device = lambda r, c: r * cols_n + c
    half = cols_n
    rows_n = 2 * cols_n
    ways = []
    for flip in (0, 1):
        pairs = [
            (device(r, c), device(c + half * ((r % 2) ^ flip), r // 2))
            for r in range(rows_n)
            for c in range(cols_n)
        ]
        ways.append(lax.ppermute(mine, EVERYWHERE, pairs))
    lower = row < half
    return jnp.concatenate(
        [jnp.where(lower, ways[0], ways[1]), jnp.where(lower, ways[1], ways[0])], 0
    )


def tied_attention(across, qkv, core, bias, sum_axes, pass_axes):
    own, other = call(
        functools.partial(logits_kernel, across),
        (shape((HALF, LENGTH), F32), shape((HALF, LENGTH), BF16)),
        [SMEM, VMEM],
        [
            pltpu.VMEM((LENGTH, 5 * LANES), BF16),
            pltpu.VMEM((LENGTH, 5 * LANES), BF16),
            pltpu.VMEM((LENGTH, LENGTH), F32),
        ],
    )(core, qkv)
    parts = call(join_kernel, shape((16, BLOCK, LENGTH), BF16), [VMEM] * 2)(own, swap_cores(other))
    weights = call(softmax_kernel, shape((16, BLOCK, LENGTH), BF16), [VMEM] * 2)(
        exchange(parts, sum_axes), bias
    )
    own = exchange(weights, sum_axes)[:OWNERS]
    other = swap_cores(own)
    mixed = call(
        functools.partial(mix_kernel, across),
        shape((qkv.shape[0],) + qkv.shape[2:], BF16),
        [SMEM, VMEM, VMEM, VMEM],
        [pltpu.VMEM((LENGTH, LENGTH), BF16), pltpu.VMEM((LENGTH, 5 * LANES), BF16)],
    )(core, own, other, qkv)
    return exchange(mixed, pass_axes)


def shards(
    pair, pair_mask, node_state, coords, neighbours, atom_type, type_table, node_query, node_key,
    node_value, edge_pair, edge_radial, node_out_w, coord_gain, radial_pair, row_gain, row_query,
    row_key, row_value, row_gate, row_out, row_bias, column_gain, column_query, column_key,
    column_value, column_gate, column_out, column_bias,
):
    rows_n, cols_n, channels = pair.shape
    row, col = lax.axis_index(("x", "y")), lax.axis_index(("z", "core"))
    core = lax.axis_index("core")[None].astype(jnp.int32)
    node_width = node_state.shape[1]
    onehot = (atom_type[:, None] == jnp.arange(type_table.shape[0], dtype=jnp.int32)[None, :])
    features = node_state + jnp.dot(onehot.astype(F32), type_table, precision=PRECISE)
    spare = LANES - node_width
    near = jnp.concatenate(
        [features, coords.T, jnp.zeros((rows_n, spare - coords.shape[0]), F32)], 1
    )
    far = column_tokens(near, row, 8)
    wq = jnp.pad(node_query * 0.25, ((0, spare), (0, spare)))
    wkv = jnp.pad(jnp.concatenate([node_key, node_value], 1), ((0, spare), (0, 0)))
    er = jnp.pad(edge_radial, ((0, LANES - edge_radial.shape[0]), (0, 0)))
    wo = jnp.pad(node_out_w, ((spare, 0), (0, spare)))
    start = (col * cols_n)[None].astype(jnp.int32)
    part = call(
        graph_kernel,
        shape((ROWS, LANES), F32),
        [SMEM, SMEM] + [VMEM] * 8,
        [pltpu.VMEM((ROWS, LANES), F32)],
    )(start, coords, pair, near, far, neighbours, wq, wkv, edge_pair, er)
    parts = exchange(jnp.broadcast_to(part[None], (8,) + part.shape), ("z", "core"))
    updated = call(merge_kernel, shape((ROWS, LANES), F32), [SMEM] + [VMEM] * 3)(
        coord_gain, parts, near, wo
    )
    new_state = updated[:, :node_width]
    new_coords = updated[:, node_width : node_width + 3].T
    far = column_tokens(updated, row, 8)
    all_xyz = lax.all_gather(new_coords, ("x", "y"), axis=1, tiled=True)

    groups = ROWS // 4
    projected = lambda count, size: [
        shape((ROWS, COLS, CH), BF16),
        shape((count, 3, size, LANES), BF16),
    ]
    x, qkv, gate = call(
        row_start_kernel,
        (*projected(8, 400), shape((HEADS, 2, 400, LANES), F32)),
        [SMEM] + [VMEM] * 9,
        [
            pltpu.VMEM((groups * COLS, 4 * CH), BF16),
            pltpu.VMEM((4 * CH, 4 * HEADS * LANES), BF16),
        ],
    )(
        new_coords, pair, far, pair_mask.T.astype(BF16), radial_pair, row_gain[None],
        row_query, row_key, row_value, row_gate,
    )

    def bias(weight, head, place):
        first = core[0] * HALF + jnp.minimum(place, OWNERS - 1) * BLOCK
        tokens = lax.dynamic_slice_in_dim(all_xyz, first, BLOCK, 1).T
        return call(bias_kernel, shape((BLOCK, LENGTH), F32), [SMEM, VMEM, VMEM])(
            lax.dynamic_index_in_dim(weight, head, 1, keepdims=False), tokens, all_xyz
        )

    row_biases = bias(row_bias, lax.axis_index("z"), row)
    column_biases = bias(column_bias, lax.axis_index("x"), lax.axis_index(("y", "z")))
    mixed = tied_attention(
        COLS, exchange(qkv, ("z", "core")), core, row_biases, ("x", "y"), ("z", "core")
    )
    x, qkv, gate = call(
        column_start_kernel,
        (*projected(16, 208), shape((HEADS, 4, 200, LANES), F32)),
        [VMEM] * 10,
        [
            pltpu.VMEM((ROWS * COLS, CH), F32),
            pltpu.VMEM((HEADS * LANES, 4 * CH), BF16),
            pltpu.VMEM((4 * CH, 4 * HEADS * LANES), BF16),
        ],
    )(
        x, gate, mixed.reshape(8, 400, LANES), pair_mask.astype(BF16), row_out,
        column_gain[None], column_query, column_key, column_value, column_gate,
    )
    mixed = tied_attention(
        ROWS, exchange(qkv, ("x", "y")), core, column_biases, ("y", "z"), ("x", "y")
    )
    pair_out = call(
        finish_kernel,
        shape((ROWS, COLS, CH), BF16),
        [VMEM] * 4,
        [
            pltpu.VMEM((ROWS * COLS, CH), F32),
            pltpu.VMEM((HEADS * LANES, 4 * CH), BF16),
        ],
    )(x, gate, mixed, column_out)
    return (pair_out, new_state, new_coords)


def solution(mesh):
    cube = Mesh(mesh.devices.reshape(4, 4, 4, 2), EVERYWHERE)
    row, col = ("x", "y"), ("z", "core")
    placed = (
        P(row, col, None), P(row, col), P(row, None), P(None, row), P(row, None), P(row),
    ) + (P(),) * 23
    return jax.shard_map(
        shards,
        mesh=cube,
        in_specs=placed,
        out_specs=(P(row, col, None), P(row, None), P(None, row)),
        check_vma=False,
    )
```

time: 674 us -> 280 us (0.42); the launches traced: 663 us -> 278 us
  waiting for transfers between devices: 311 us -> 38 us
  local copies, waits for them, and re-layouts: 122 us -> 11.6 us
  matrix products: 80.3 us -> 0.96 us
  Pallas kernels: 0 us -> 38.5 us
  blocking collectives: 118 us -> 153 us
  starting transfers between devices: 0.71 us -> 33 us
  between operations: 15.3 us -> 1.17 us
  other arithmetic: 14.5 us -> 1.73 us
    all_gather x4 -> x0, waiting for transfers between devices: 190 us -> none  [the longest x1 73.6 us: column_pass(): key_piece = lax.all_gather(key_rows, 'row', axis=0, tiled=True)]
    all_to_all x0 -> x5, blocking collectives: none -> 126 us  [exchange(): return lax.all_to_all(parts, axes, split_axis=0, concat_axis=0, tiled=True)]
    psum x2 -> x0, waiting for transfers between devices: 121 us -> none  [the longest x1 79.3 us: row_pass(): summed = lax.psum(partial_value, 'row')]
    all_gather x7 -> x1, blocking collectives: 118 us -> 27.1 us  [shards(): all_xyz = lax.all_gather(new_coords, ('x', 'y'), axis=1, tiled=True)]
    dot_general x32 -> x1, matrix products: 80.3 us -> 0.96 us  [shards(): jnp.dot(onehot.astype(F32), type_table, precision=PRECISE)]
    all_gather x6 -> x1, local copies, waits for them, and re-layouts: 61.4 us -> 0.01 us  [shards(): all_xyz = lax.all_gather(new_coords, ('x', 'y'), axis=1, tiled=True)]
    pallas_call x0 -> x15, Pallas kernels: none -> 38.5 us  [the longest x1 9.21 us: shards(): call(graph_kernel, shape((ROWS, LANES), F32), [SMEM, SMEM] + [VMEM] * 8,...]
    gather x7 -> x0, local copies, waits for them, and re-layouts: 31.4 us -> none  [the longest x1 13.8 us: shards(): pair_rows = pair[jnp.arange(rows_n)[:, None], local_index]]
  transfers between devices with their start and end apart: 6 -> 12, of which waited for: 6 -> 8; matrix products, arithmetic and copies ran while one was open for 17% -> 2% of each run, Pallas kernels for 0% -> 1%
where the time goes in v1:
time: 280 us; the launch traced here: 278 us
  blocking collectives  153 us (55%)
  Pallas kernels  38.5 us (14%)
  waiting for transfers between devices  38 us (14%)
  starting transfers between devices  33 us (12%)
  local copies, waits for them, and re-layouts  11.6 us (4%)
    all_to_all x5, blocking collectives, exchange(): return lax.all_to_all(parts, axes, split_axis=0, concat_axis=0, tiled=True)  126 us
    all_to_all x4, waiting for transfers between devices, exchange(): return lax.all_to_all(parts, axes, split_axis=0, concat_axis=0, tiled=True)  29.8 us
    all_gather x1, blocking collectives, shards(): all_xyz = lax.all_gather(new_coords, ('x', 'y'), axis=1, tiled=True)  27.1 us
    all_to_all x4, starting transfers between devices, exchange(): return lax.all_to_all(parts, axes, split_axis=0, concat_axis=0, tiled=True)  18.1 us
    ppermute x4, starting transfers between devices, column_tokens(): ways.append(lax.ppermute(mine, EVERYWHERE, pairs))  14.6 us
    pallas_call x1, Pallas kernels, shards(): call(graph_kernel, shape((ROWS, LANES), F32), [SMEM, SMEM] + [VMEM] * 8,...  9.21 us
    pallas_call x1, Pallas kernels, shards(): call(row_start_kernel, (*projected(8, 400), shape((HEADS, 2, 400, LANES),...  8.45 us
    ppermute x4, waiting for transfers between devices, swap_cores(): return lax.ppermute(x, 'core', [(0, 1), (1, 0)])  6.93 us
  transfers between devices with their start and end apart: 12, of which 8 were waited for; matrix products, arithmetic and copies ran while one was open for 2% of the time, Pallas kernels for 1%

profile of v1, /device:TPU:0, one launch (start us, length us, event | category | flops | bytes accessed | tf_op | source)
XLA Modules:
  0.0 278.2 jit_solution(16977740020808000139)
XLA Ops:
  3.3 8.2 %collective-permute-start.1 = (f32[40,128]{1,0:T(8,128)S(1)}, f32[40,128]{1,0:T(8,128)S(1)}, u32[]{:S(2)}, u32[]{:S(2)}) collective-permute-start(f32[40,128]{1,0:T(8,128)S(1)} %maximum_maximum_fusion.near_ref), channel_id=1, source_target_pairs={{0,64},{1,72},{2,80},{3,88},{4,96},{5,104},{6,112},{7,120},{8,0},{... | collective-permute-start | bytes 61448 | tf_op jit(solution)/shard_map/ppermute | solution.py:441
  17.3 9.2 %shard_map.292 = f32[40,128]{1,0:T(8,128)S(1)} custom-call(s32[1]{0:T(128)} %bitcast.start_ref, f32[3,40]{1,0:T(4,128)S(1)} %copy-done.25, bf16[40,80,128]{2,1,0:T(8,128)(2,1)S(1)} %copy-done.1, f32[40,128]{1,0:T(8,128)S(1)} %maximum_maximum_fusion.near_ref, f32[80,128]{1,0:T(8,128)S(1)} %pad_maximum_fusion.far_ref, s32[40,64]{1,0:T(8,128)S(1)} %copy-done.23, ...), custom_call_target="tpu_custom_call" | custom-call | tf_op jit(solution)/shard_map/pallas_call | solution.py:496
  27.2 7.1 %all-to-all-start = ((f32[8,40,128]{2,1,0:T(8,128)}), f32[8,40,128]{2,1,0:T(8,128)S(1)}, u32[]{:S(2)}, u32[]{:S(2)}) async-start(f32[8,40,128]{2,1,0:T(8,128)} %broadcast_in_dim.25), calls=%async_computation | async-start | bytes 327680 | tf_op jit(solution)/shard_map/all_to_all | solution.py:423
  35.0 5.7 %all-to-all-done.parts_ref = f32[8,40,128]{2,1,0:T(8,128)S(1)} async-done(((f32[8,40,128]{2,1,0:T(8,128)}), f32[8,40,128]{2,1,0:T(8,128)S(1)}, u32[]{:S(2)}, u32[]{:S(2)}) %all-to-all-start) | async-done | bytes 163872 | tf_op jit(solution)/shard_map/all_to_all | solution.py:423
  40.8 2.1 shard_map.293
  44.3 4.3 %collective-permute-start.3 = (f32[40,128]{1,0:T(8,128)}, f32[40,128]{1,0:T(8,128)S(1)}, u32[]{:S(2)}, u32[]{:S(2)}) collective-permute-start(f32[40,128]{1,0:T(8,128)} %shard_map.293), channel_id=1, source_target_pairs={{0,64},{1,72},{2,80},{3,88},{4,96},{5,104},{6,112},{7,120},{8,0},{... | collective-permute-start | bytes 61448 | tf_op jit(solution)/shard_map/ppermute | solution.py:441
  50.9 8.5 %shard_map.294 = (bf16[40,80,128]{2,1,0:T(8,128)(2,1)S(1)}, bf16[8,3,400,128]{3,2,1,0:T(8,128)(2,1)S(1)}, f32[4,2,400,128]{3,2,1,0:T(8,128)S(1)}) custom-call(f32[3,40]{1,0:T(4,128)S(1)} %bitcast.20, bf16[40,80,128]{2,1,0:T(8,128)(2,1)S(1)} %copy-done.2, f32[80,128]{1,0:T(8,128)S(1)} %pad_maximum_fusion.1.far_ref, bf16[80,40]{1,0:T(8,128)(2,1)S(1)} %copy.40.mask_ref, ...), custom_call_target="tpu_custom_call" | custom-call | tf_op jit(solution)/shard_map/pallas_call | solution.py:516
  59.4 41.2 %all_to_all.45.qkv_ref = bf16[8,3,400,128]{3,2,1,0:T(8,128)(2,1)S(1)} all-to-all(bf16[8,3,400,128]{3,2,1,0:T(8,128)(2,1)S(1)} %get-tuple-element.15), channel_id=1, replica_groups=mesh['x'=4,'y'=4,'z'=4,'core'=2] {'z','core'}, dimensions={0} | all-to-all | bytes 4915200 | tf_op jit(solution)/shard_map/all_to_all | solution.py:423
  102.2 1.7 collective-permute-done.4.other_ref
  104.9 3.7 %all-to-all-start.2 = ((bf16[16,32,640]{2,1,0:T(8,128)(2,1)}), bf16[16,32,640]{2,1,0:T(8,128)(2,1)S(1)}, u32[]{:S(2)}, u32[]{:S(2)}) async-start(bf16[16,32,640]{2,1,0:T(8,128)(2,1)} %shard_map.296), calls=%async_computation.2 | async-start | bytes 1310720 | tf_op jit(solution)/shard_map/all_to_all | solution.py:423
  109.3 27.1 %all-gather = f32[16,40,3]{1,2,0:T(4,128)S(1)} all-gather(f32[1,40,3]{1,2,0:T(4,128)S(1)} %bitcast.21), channel_id=1, replica_groups=mesh['x'=4,'y'=4,'z'=4,'core'=2] {'x','y'}, dimensions={0}, use_global_device_ids=true | all-gather | bytes 8160 | tf_op jit(solution)/shard_map/all_gather | solution.py:509
  136.6 1.9 shard_map.297.bias_ref
  138.8 14.8 %all_to_all.46 = bf16[16,32,640]{2,1,0:T(8,128)(2,1)S(1)} all-to-all(bf16[16,32,640]{2,1,0:T(8,128)(2,1)S(1)} %shard_map.298), channel_id=1, replica_groups=mesh['x'=4,'y'=4,'z'=4,'core'=2] {'x','y'}, dimensions={0} | all-to-all | bytes 1310720 | tf_op jit(solution)/shard_map/all_to_all | solution.py:423
  155.6 2.0 shard_map.299
  157.6 3.7 %all-to-all-start.4 = ((bf16[8,400,128]{2,1,0:T(8,128)(2,1)}), bf16[8,400,128]{2,1,0:T(8,128)(2,1)S(1)}, u32[]{:S(2)}, u32[]{:S(2)}) async-start(bf16[8,400,128]{2,1,0:T(8,128)(2,1)} %shard_map.299), calls=%async_computation.4 | async-start | bytes 1638400 | tf_op jit(solution)/shard_map/all_to_all | solution.py:423
  161.3 13.2 %all-to-all-done.4.mixed_ref = bf16[8,400,128]{2,1,0:T(8,128)(2,1)S(1)} async-done(((bf16[8,400,128]{2,1,0:T(8,128)(2,1)}), bf16[8,400,128]{2,1,0:T(8,128)(2,1)S(1)}, u32[]{:S(2)}, u32[]{:S(2)}) %all-to-all-start.4) | async-done | bytes 819232 | tf_op jit(solution)/shard_map/all_to_all | solution.py:423
  176.1 4.4 %shard_map.300 = (bf16[40,80,128]{2,1,0:T(8,128)(2,1)S(1)}, bf16[16,3,208,128]{3,2,1,0:T(8,128)(2,1)S(1)}, f32[4,4,200,128]{3,2,1,0:T(8,128)S(1)}) custom-call(bf16[40,80,128]{2,1,0:T(8,128)(2,1)S(1)} %copy-done.8, f32[4,2,400,128]{3,2,1,0:T(8,128)S(1)} %copy-done.4, bf16[8,400,128]{2,1,0:T(8,128)(2,1)S(1)} %all-to-all-done.4.mixed_ref, ...), custom_call_target="tpu_custom_call" | custom-call | tf_op jit(solution)/shard_map/pallas_call | solution.py:541
  181.4 36.4 %all_to_all.47.qkv_ref = bf16[16,3,208,128]{3,2,1,0:T(8,128)(2,1)S(1)} all-to-all(bf16[16,3,208,128]{3,2,1,0:T(8,128)(2,1)S(1)} %get-tuple-element.20), channel_id=1, replica_groups=mesh['x'=4,'y'=4,'z'=4,'core'=2] {'x','y'}, dimensions={0} | all-to-all | bytes 5111808 | tf_op jit(solution)/shard_map/all_to_all | solution.py:423
  222.1 3.6 %all-to-all-start.6 = ((bf16[16,32,640]{2,1,0:T(8,128)(2,1)}), bf16[16,32,640]{2,1,0:T(8,128)(2,1)S(1)}, u32[]{:S(2)}, u32[]{:S(2)}) async-start(bf16[16,32,640]{2,1,0:T(8,128)(2,1)} %shard_map.302), calls=%async_computation.6 | async-start | bytes 1310720 | tf_op jit(solution)/shard_map/all_to_all | solution.py:423
  226.5 1.9 shard_map.303.bias_ref
  228.4 10.9 %all-to-all-done.6.parts_ref = bf16[16,32,640]{2,1,0:T(8,128)(2,1)S(1)} async-done(((bf16[16,32,640]{2,1,0:T(8,128)(2,1)}), bf16[16,32,640]{2,1,0:T(8,128)(2,1)S(1)}, u32[]{:S(2)}, u32[]{:S(2)}) %all-to-all-start.6) | async-done | bytes 655392 | tf_op jit(solution)/shard_map/all_to_all | solution.py:423
  239.5 15.5 %all_to_all.48 = bf16[16,32,640]{2,1,0:T(8,128)(2,1)S(1)} all-to-all(bf16[16,32,640]{2,1,0:T(8,128)(2,1)S(1)} %shard_map.304), channel_id=1, replica_groups=mesh['x'=4,'y'=4,'z'=4,'core'=2] {'y','z'}, dimensions={0} | all-to-all | bytes 1310720 | tf_op jit(solution)/shard_map/all_to_all | solution.py:423
  258.1 18.2 %all_to_all.49.mixed_ref = bf16[16,208,128]{2,1,0:T(8,128)(2,1)S(1)} all-to-all(bf16[16,208,128]{2,1,0:T(8,128)(2,1)S(1)} %shard_map.305), channel_id=1, replica_groups=mesh['x'=4,'y'=4,'z'=4,'core'=2] {'x','y'}, dimensions={0} | all-to-all | bytes 1703936 | tf_op jit(solution)/shard_map/all_to_all | solution.py:423
  276.3 1.9 shard_map.306
  (110 shorter events, 29.7 us)
Async XLA Ops:
  0.6 40.1 %copy-start.26 = (f32[4]{0:T(128)S(1)}, f32[4]{0:T(128)}, u32[]{:S(2)}) copy-start(f32[4]{0:T(128)} %gain_ref.1) | copy-start | bytes 52
  0.7 47.9 %copy-start.29 = (s32[40,80]{1,0:T(8,128)S(1)}, s32[40,80]{1,0:T(8,128)}, u32[]{:S(2)}) copy-start(s32[40,80]{1,0:T(8,128)} %param.30) | copy-start | bytes 38404
  0.7 50.1 %copy-start.27 = (f32[128]{0:T(128)S(1)}, f32[128]{0:T(128)}, u32[]{:S(2)}) copy-start(f32[128]{0:T(128)} %param.44) | copy-start | bytes 1540
  0.7 50.1 %copy-start.18 = (f32[64,128]{1,0:T(8,128)S(1)}, f32[64,128]{1,0:T(8,128)}, u32[]{:S(2)}) copy-start(f32[64,128]{1,0:T(8,128)} %radial_ref.1) | copy-start | bytes 98308
  0.7 50.1 %copy-start.19 = (bf16[128,128]{1,0:T(8,128)(2,1)S(1)}, bf16[128,128]{1,0:T(8,128)(2,1)}, u32[]{:S(2)}) copy-start(bf16[128,128]{1,0:T(8,128)(2,1)} %wq_ref.2) | copy-start | bytes 98308
  0.7 50.1 %copy-start.20 = (bf16[128,128]{1,0:T(8,128)(2,1)S(1)}, bf16[128,128]{1,0:T(8,128)(2,1)}, u32[]{:S(2)}) copy-start(bf16[128,128]{1,0:T(8,128)(2,1)} %wk_ref.2) | copy-start | bytes 98308
  0.7 50.1 %copy-start.21 = (bf16[128,128]{1,0:T(8,128)(2,1)S(1)}, bf16[128,128]{1,0:T(8,128)(2,1)}, u32[]{:S(2)}) copy-start(bf16[128,128]{1,0:T(8,128)(2,1)} %wv_ref.2) | copy-start | bytes 98308
  0.7 50.1 %copy-start.22 = (bf16[128,128]{1,0:T(8,128)(2,1)S(1)}, bf16[128,128]{1,0:T(8,128)(2,1)}, u32[]{:S(2)}) copy-start(bf16[128,128]{1,0:T(8,128)(2,1)} %wg_ref.2) | copy-start | bytes 98308
  2.7 11.3 %collective-permute-start = (f32[40,128]{1,0:T(8,128)S(1)}, f32[40,128]{1,0:T(8,128)S(1)}, u32[]{:S(2)}, u32[]{:S(2)}) collective-permute-start(f32[40,128]{1,0:T(8,128)S(1)} %maximum_maximum_fusion.near_ref), channel_id=1, source_target_pairs={{0,0},{1,8},{2,16},{3,24},{4,32},{5,40},{6,48},{7,56},{8,64},{9,72... | collective-permute-start | bytes 61448 | tf_op jit(solution)/shard_map/ppermute | solution.py:441
  3.3 10.6 %collective-permute-start.1 = (f32[40,128]{1,0:T(8,128)S(1)}, f32[40,128]{1,0:T(8,128)S(1)}, u32[]{:S(2)}, u32[]{:S(2)}) collective-permute-start(f32[40,128]{1,0:T(8,128)S(1)} %maximum_maximum_fusion.near_ref), channel_id=1, source_target_pairs={{0,64},{1,72},{2,80},{3,88},{4,96},{5,104},{6,112},{7,120},{8,0},{... | collective-permute-start | bytes 61448 | tf_op jit(solution)/shard_map/ppermute | solution.py:441
  27.2 13.5 %all-to-all-start = ((f32[8,40,128]{2,1,0:T(8,128)}), f32[8,40,128]{2,1,0:T(8,128)S(1)}, u32[]{:S(2)}, u32[]{:S(2)}) async-start(f32[8,40,128]{2,1,0:T(8,128)} %broadcast_in_dim.25), calls=%async_computation | async-start | bytes 327680 | tf_op jit(solution)/shard_map/all_to_all | solution.py:423
  42.9 6.7 %collective-permute-start.2 = (f32[40,128]{1,0:T(8,128)}, f32[40,128]{1,0:T(8,128)S(1)}, u32[]{:S(2)}, u32[]{:S(2)}) collective-permute-start(f32[40,128]{1,0:T(8,128)} %shard_map.293), channel_id=1, source_target_pairs={{0,0},{1,8},{2,16},{3,24},{4,32},{5,40},{6,48},{7,56},{8,64},{9,72... | collective-permute-start | bytes 61448 | tf_op jit(solution)/shard_map/ppermute | solution.py:441
  44.3 6.5 %collective-permute-start.3 = (f32[40,128]{1,0:T(8,128)}, f32[40,128]{1,0:T(8,128)S(1)}, u32[]{:S(2)}, u32[]{:S(2)}) collective-permute-start(f32[40,128]{1,0:T(8,128)} %shard_map.293), channel_id=1, source_target_pairs={{0,64},{1,72},{2,80},{3,88},{4,96},{5,104},{6,112},{7,120},{8,0},{... | collective-permute-start | bytes 61448 | tf_op jit(solution)/shard_map/ppermute | solution.py:441
  49.6 59.7 %copy-start.24 = (f32[40,3]{0,1:T(4,128)}, f32[40,3]{0,1:T(4,128)S(1)}, u32[]{:S(2)}) copy-start(f32[40,3]{0,1:T(4,128)S(1)} %copy.44) | copy-start | bytes 1444
  59.3 41.2 %copy-start.3 = (f32[4,2,400,128]{3,2,1,0:T(8,128)}, f32[4,2,400,128]{3,2,1,0:T(8,128)S(1)}, u32[]{:S(2)}) copy-start(f32[4,2,400,128]{3,2,1,0:T(8,128)S(1)} %get-tuple-element.14.gate_ref) | copy-start | bytes 4915204
  59.3 41.2 %copy-start.7 = (bf16[40,80,128]{2,1,0:T(8,128)(2,1)}, bf16[40,80,128]{2,1,0:T(8,128)(2,1)S(1)}, u32[]{:S(2)}) copy-start(bf16[40,80,128]{2,1,0:T(8,128)(2,1)S(1)} %get-tuple-element.13.x_ref) | copy-start | bytes 2457604
  102.1 1.8 collective-permute-start.4
  104.9 33.7 %all-to-all-start.2 = ((bf16[16,32,640]{2,1,0:T(8,128)(2,1)}), bf16[16,32,640]{2,1,0:T(8,128)(2,1)S(1)}, u32[]{:S(2)}, u32[]{:S(2)}) async-start(bf16[16,32,640]{2,1,0:T(8,128)(2,1)} %shard_map.296), calls=%async_computation.2 | async-start | bytes 1310720 | tf_op jit(solution)/shard_map/all_to_all | solution.py:423
  153.8 1.8 collective-permute-start.5
  157.6 17.0 %all-to-all-start.4 = ((bf16[8,400,128]{2,1,0:T(8,128)(2,1)}), bf16[8,400,128]{2,1,0:T(8,128)(2,1)S(1)}, u32[]{:S(2)}, u32[]{:S(2)}) async-start(bf16[8,400,128]{2,1,0:T(8,128)(2,1)} %shard_map.299), calls=%async_computation.4 | async-start | bytes 1638400 | tf_op jit(solution)/shard_map/all_to_all | solution.py:423
  181.4 36.4 %copy-start.5 = (f32[4,4,200,128]{3,2,1,0:T(8,128)}, f32[4,4,200,128]{3,2,1,0:T(8,128)S(1)}, u32[]{:S(2)}) copy-start(f32[4,4,200,128]{3,2,1,0:T(8,128)S(1)} %get-tuple-element.19.gate_ref) | copy-start | bytes 4915204
  219.3 1.8 collective-permute-start.6
  222.1 17.2 %all-to-all-start.6 = ((bf16[16,32,640]{2,1,0:T(8,128)(2,1)}), bf16[16,32,640]{2,1,0:T(8,128)(2,1)S(1)}, u32[]{:S(2)}, u32[]{:S(2)}) async-start(bf16[16,32,640]{2,1,0:T(8,128)(2,1)} %shard_map.302), calls=%async_computation.6 | async-start | bytes 1310720 | tf_op jit(solution)/shard_map/all_to_all | solution.py:423
  255.1 1.8 collective-permute-start.7
  (18 other events, 249.9 us)

commit v2 on v1

v2 whole, which is shorter than its diff:
```python
import functools
import math

import jax
import jax.numpy as jnp
from jax import lax
from jax.experimental import pallas as pl
from jax.experimental.pallas import tpu as pltpu
from jax.sharding import Mesh
from jax.sharding import PartitionSpec as P

BF16 = jnp.bfloat16
F32 = jnp.float32
PRECISE = lax.Precision.HIGHEST
RADIAL_REACH = 24.0
NEGATIVE = -1e30
EVERYWHERE = ("x", "y", "z", "core")

VMEM = pl.BlockSpec(memory_space=pltpu.VMEM)
SMEM = pl.BlockSpec(memory_space=pltpu.SMEM)
MIB = 1024 * 1024

ROWS, COLS, CH, HEADS = 40, 80, 128, 4
LENGTH = 640
LANES = 128
SLOT = 32
BLOCK = 24
OWNERS = 14
HALF = LENGTH // 2


def call(kernel, out_shape, in_specs, scratch=(), limit=44):
    out_specs = jax.tree.map(lambda _: VMEM, out_shape)
    return pl.pallas_call(
        kernel,
        out_shape=out_shape,
        in_specs=in_specs,
        out_specs=out_specs,
        scratch_shapes=list(scratch),
        compiler_params=pltpu.CompilerParams(vmem_limit_bytes=limit * MIB),
    )


def shape(dims, dtype):
    return jax.ShapeDtypeStruct(dims, dtype)


def iota(dims, axis):
    return lax.broadcasted_iota(jnp.int32, dims, axis)


def dot(a, b):
    return jnp.dot(a, b, preferred_element_type=F32)


def dot32(a, b):
    return jnp.dot(a, b, preferred_element_type=F32, precision=PRECISE)


def length_of(square):
    square = square + 1e-06
    return square * lax.rsqrt(square)


def split(a):
    high = a.astype(BF16)
    return high, (a - high.astype(F32)).astype(BF16)


def split3(a):
    high, low = split(a)
    return high, low, (a - high.astype(F32) - low.astype(F32)).astype(BF16)


def graph_kernel(
    place_ref, xyz_ref, near_ref, way0_ref, way1_ref, pair_ref, neigh_ref, wq_ref, wk_ref, wv_ref,
    ep_ref, er_ref, small_ref, values_ref, q_ref, sums_ref,
):
    step = 8
    bins = 64
    lower = place_ref[1] == 1
    way0, way1 = way0_ref[...], way1_ref[...]
    far = jnp.concatenate([jnp.where(lower, way0, way1), jnp.where(lower, way1, way0)], 0)
    blank = jnp.zeros((64, LANES), F32)
    wq = jnp.concatenate([wq_ref[...] * 0.25, jnp.zeros((64, 64), F32)], 1)
    q_ref[...] = dot32(near_ref[...], jnp.concatenate([wq, blank], 0))
    wkv = jnp.concatenate([wk_ref[...], wv_ref[...]], 1)
    base = dot32(far, jnp.concatenate([wkv, blank], 0))
    far_xyz = [jnp.broadcast_to(far[:, 64 + c : 65 + c], (COLS, LANES)) for c in range(3)]
    lane = iota((1, LANES), 1)
    centers = (lane % bins).astype(F32) * (RADIAL_REACH / (bins - 1))
    width = bins / RADIAL_REACH
    of_lane, to_lane = iota((LANES, LANES), 0), iota((LANES, LANES), 1)
    to_value = (of_lane < 64) & (of_lane // 16 == (to_lane % 64) // 16)
    to_small = (of_lane < 64) & (of_lane // 16 == jnp.minimum(to_lane % 24 // 5, 3))
    head_sum = jnp.concatenate(
        [jnp.where(to_value, 1.0, 0.0), jnp.where(to_small, 1.0, 0.0)], 1
    ).astype(BF16)
    head_sum = jnp.concatenate([head_sum] * 3, 0)
    table_high, table_low = split(er_ref[...])
    table = jnp.concatenate([table_high, table_high, table_low, jnp.zeros_like(table_low)], 0)
    ones = jnp.ones((64, LANES), BF16)
    cell = iota((COLS, 64), 0) + place_ref[0]
    place = lane % 24
    slot = jnp.where(place < 20, place % 5, place - 15)

    def some(block, small):
        first = pl.multiple_of(block * step, step)
        offsets, bases, counts, queries = [], [], [], []
        neigh = neigh_ref[pl.ds(first, step), :]
        q_some = q_ref[pl.ds(first, step), :]
        for u in range(step):
            off = [far_xyz[c] - xyz_ref[c, first + u] for c in range(3)]
            spacing = length_of(off[0] * off[0] + off[1] * off[1] + off[2] * off[2])
            away = (spacing - centers) * width
            bases.append(jnp.exp(-(away * away)))
            offsets.append(off)
            counts.append(jnp.where(cell == neigh[u : u + 1, :], 1.0, 0.0).astype(BF16))
            queries.append(q_some[u : u + 1, :])
        cells = pair_ref[pl.ds(first, step)].reshape(step * COLS, CH)
        high, low = split(jnp.concatenate(bases, 0))
        bases = jnp.concatenate([jnp.where(lane < bins, high, low), high], 1)
        edge = dot(cells, ep_ref[...]) + dot(bases, table)
        count = dot(jnp.concatenate(counts, 0), ones)
        edges, products = [], []
        for u in range(step):
            one = edge[u * COLS : (u + 1) * COLS] + base
            edges.append(one)
            products.append(one * queries[u])
        scores = dot(jnp.concatenate(split3(jnp.concatenate(products, 0)), 1), head_sum)
        lines, sums = [], []
        for u in range(step):
            times = count[u * COLS : (u + 1) * COLS]
            score = scores[u * COLS : (u + 1) * COLS]
            both = []
            for part in (score[:, :LANES], score[:, LANES:]):
                part = jnp.where(times > 0.0, part, NEGATIVE)
                top = jnp.max(part, axis=0, keepdims=True)
                both.append((top, times * jnp.exp(part - top)))
            (_, for_value), (top, w) = both
            sums.append(jnp.sum(for_value * edges[u], axis=0, keepdims=True))
            entries = [top, jnp.sum(w, axis=0, keepdims=True)]
            entries += [jnp.sum(w * offsets[u][c], axis=0, keepdims=True) for c in range(3)]
            entries += [xyz_ref[c, first + u] for c in range(3)]
            line = jnp.zeros((1, LANES), F32)
            for at, entry in enumerate(entries):
                line = jnp.where(slot == at, entry, line)
            lines.append(line)
        sums_ref[pl.ds(first, step), :] = jnp.concatenate(sums, 0)
        return jnp.where(lane // 24 == block, jnp.concatenate(lines, 0), small)

    small = lax.fori_loop(0, ROWS // step, some, jnp.zeros((step, LANES), F32))
    small_ref[...] = jnp.broadcast_to(small[None], small_ref.shape)
    sums = sums_ref[...]
    turned = pltpu.roll(sums, 64, 1)
    high = turned.astype(BF16).astype(F32)
    low = sums - sums.astype(BF16).astype(F32)
    values = jnp.where(lane < 64, high, low)
    values_ref[...] = jnp.concatenate([values, jnp.zeros((8, LANES), F32)], 0).astype(BF16)


def merge_kernel(gain_ref, parts_ref, out_ref):
    of_lane, to_lane = iota((LANES, LANES), 0), iota((LANES, LANES), 1)
    first = jnp.where(to_lane < 120, to_lane // 24 * 24, 0)
    home = first + jnp.minimum(to_lane % 24 // 5, 3) * 5
    to_top = jnp.where(of_lane == home, 1.0, 0.0).astype(BF16)
    to_total = jnp.where(of_lane == home + 1, 1.0, 0.0)
    start = to_lane // 3 * 24
    gain = jnp.zeros((LANES, LANES), F32)
    for head in range(4):
        at = (of_lane == start + head * 5 + 2 + to_lane % 3) & (to_lane < 15)
        gain = jnp.where(at, gain_ref[head], gain)
    to_old = jnp.where((of_lane == start + 20 + to_lane % 3) & (to_lane < 15), 1.0, 0.0)
    parts = parts_ref[...].reshape(128 * 8, LANES)
    tops = dot(jnp.concatenate(split3(parts), 1), jnp.concatenate([to_top] * 3, 0))
    merged, old = [], []
    for row in range(16):
        some = [slice((row * 8 + p) * 8, (row * 8 + p + 1) * 8) for p in range(8)]
        highest = functools.reduce(jnp.maximum, [tops[at] for at in some])
        merged.append(sum(jnp.exp(tops[at] - highest) * parts[at] for at in some))
        old.append(parts[some[0]])
    merged = jnp.concatenate(merged, 0)
    ratio = merged / dot32(merged, to_total)
    new = dot32(jnp.concatenate(old, 0), to_old) + dot32(ratio, gain)
    out_ref[...] = new.reshape(16, 8, LANES)


def node_kernel(place_ref, parts_ref, sent_ref, near_ref, wo_ref, out_ref):
    lane = iota((8, LANES), 1)
    of_lane, to_lane = iota((LANES, LANES), 0), iota((LANES, LANES), 1)
    parts = [parts_ref[place_ref[2] * 8 + p] for p in range(8)]
    values = [sent_ref[p, sent_ref.shape[1] - 48 :, :].astype(F32) for p in range(8)]
    values = [value + pltpu.roll(value, 64, 1) for value in values]
    stacked = jnp.concatenate(parts, 0)
    attended = []
    for g in range(5):
        home = g * 24 + (to_lane % 64) // 16 * 5 + to_lane // 64
        both = dot32(stacked, jnp.where(of_lane == home, 1.0, 0.0))
        tops = [both[p * 8 : (p + 1) * 8] for p in range(8)]
        highest = functools.reduce(jnp.maximum, tops)
        above, below = 0.0, 0.0
        for p in range(8):
            scale = jnp.exp(tops[p] - highest)
            above = above + scale * values[p][g * 8 : (g + 1) * 8]
            below = below + scale * pltpu.roll(tops[p], 64, 1)
        attended.append(jnp.where(lane < 64, above / jnp.where(lane < 64, below, 1.0), 0.0))
    attended = jnp.concatenate(attended, 0)[:, :64]
    out_ref[...] = near_ref[...][:, :64] + dot32(attended, wo_ref[...])


def widen(weight, wide_ref, column):
    weight = weight.astype(F32)
    lane = iota((CH, LANES), 1)
    for h in range(HEADS):
        for i in range(4):
            turned = pltpu.roll(weight, ((i - h) * SLOT) % LANES, 1) if i != h else weight
            wide_ref[i * CH : (i + 1) * CH, column + h * LANES : column + (h + 1) * LANES] = (
                jnp.where(lane // SLOT == i, turned, 0.0).astype(BF16)
            )


def widen_out(weight, wide_ref):
    wide_ref[...] = jnp.zeros_like(wide_ref)
    for h in range(HEADS):
        for i in range(4):
            wide_ref[
                h * LANES + i * SLOT : h * LANES + (i + 1) * SLOT, i * CH : (i + 1) * CH
            ] = weight[h * SLOT : (h + 1) * SLOT, :]


def normed(rounded, norm_gain):
    mean_of = jnp.full((CH, LANES), 1.0 / CH, BF16)
    centered = rounded.astype(F32) - dot(rounded, mean_of)
    high, low = split(centered * centered)
    spread = dot(jnp.concatenate([high, low], 1), jnp.concatenate([mean_of, mean_of], 0))
    return centered * lax.rsqrt(spread + 1e-05) * norm_gain


def spread_mask(mask, group):
    n = mask.shape[1]
    pick = iota((n, LANES), 0) == 4 * group + iota((n, LANES), 1) // SLOT
    return dot(mask, jnp.where(pick, 1.0, 0.0).astype(BF16))


def put_projections(z, mask, wide_ref, put):
    scales = (1.0 / math.sqrt(SLOT), 1.0 / math.sqrt(LENGTH))
    for matrix in range(3):
        wide = HEADS * LANES
        out = dot(z, wide_ref[:, matrix * wide : (matrix + 1) * wide])
        for h in range(HEADS):
            one = out[:, h * LANES : (h + 1) * LANES]
            if matrix < 2:
                one = one * mask * scales[matrix]
            put(matrix, h, one)


def gate_kernel(z_ref, weight_ref, gate_ref, wide_ref):
    widen(weight_ref[...], wide_ref, 0)
    for block in range(z_ref.shape[0]):
        out = jax.nn.sigmoid(dot(z_ref[block], wide_ref[...]))
        for h in range(HEADS):
            gate_ref[h, block] = out[:, h * LANES : (h + 1) * LANES].astype(BF16)


def row_start_kernel(
    place_ref, xyz_ref, new_ref, sums_ref, pair_ref, mask_ref, radial_ref, gain_ref, weights_ref,
    x_ref, qkv_ref, z_ref, wide_ref,
):
    bins = 64
    for at in range(3):
        widen(weights_ref[at * CH : (at + 1) * CH, :], wide_ref, at * HEADS * LANES)
    far = [new_ref[place_ref[0] * 2 + half] for half in range(2)]
    far_xyz = [
        jnp.concatenate(
            [
                jnp.broadcast_to(part[:, g * 3 + c : g * 3 + c + 1], (8, LANES))
                for part in far
                for g in range(5)
            ],
            0,
        )
        for c in range(3)
    ]
    row = place_ref[2]
    lane = iota((1, LANES), 1)
    centers = (lane % bins).astype(F32) * (RADIAL_REACH / (bins - 1))
    width = bins / RADIAL_REACH
    table = radial_ref[...]
    blank = jnp.zeros_like(table)
    table = jnp.concatenate(
        [jnp.concatenate([table, blank], 1), jnp.concatenate([blank, table], 1)], 0
    )
    table_high, table_low = split(table)
    table = jnp.concatenate([table_high, table_low, table_high], 0)
    norm_gain = gain_ref[...]

    together = 2
    size = ROWS // 8 * COLS

    def some(step, carry):
        bases, rows = [], []
        for at in range(2 * together):
            n = (step * together * 2 + at) * 2
            off = [
                far_xyz[c]
                - jnp.where(
                    lane < bins,
                    xyz_ref[row, n & 7, (n >> 3) * 3 + c],
                    xyz_ref[row, (n + 1) & 7, ((n + 1) >> 3) * 3 + c],
                )
                for c in range(3)
            ]
            spacing = length_of(off[0] * off[0] + off[1] * off[1] + off[2] * off[2])
            away = (spacing - centers) * width
            bases.append(jnp.exp(-(away * away)))
        high, low = split(jnp.concatenate(bases, 0))
        added = dot(jnp.concatenate([high, high, low], 1), table)
        for i in range(4 * together):
            at = (i // 2) * COLS
            n = step * together * 4 + i
            part = added[at : at + COLS, (i % 2) * CH : (i % 2 + 1) * CH]
            rows.append((pair_ref[n].astype(F32) + part).astype(BF16))
            x_ref[n] = rows[-1]
        z = normed(jnp.concatenate(rows, 0), norm_gain).astype(BF16)
        for i in range(4 * together):
            at = (step * together + i // 4) * COLS
            half, at = at // size, at % size
            z_ref[half, pl.ds(pl.multiple_of(at, COLS), COLS), (i % 4) * CH : (i % 4 + 1) * CH] = z[
                i * COLS : (i + 1) * COLS
            ]
        return carry

    groups = ROWS // 4
    lax.fori_loop(0, groups // together, some, 0)
    for s in range(2):
        for h in range(HEADS):
            qkv_ref[h * 2 + s, 3 * size :] = sums_ref[...]
        mask = jnp.concatenate(
            [spread_mask(mask_ref[...], s * (groups // 2) + g) for g in range(groups // 2)], 0
        )

        def put(matrix, h, one):
            qkv_ref[h * 2 + s, matrix * size : (matrix + 1) * size] = one.astype(BF16)

        put_projections(z_ref[s], mask, wide_ref, put)


def gathered(parts_ref, which, g, across):
    count = parts_ref.shape[0]
    if across == COLS:
        at = (which * 5 + g) * across
        return jnp.concatenate([parts_ref[p, at : at + across, :] for p in range(count)], 0)
    size = parts_ref.shape[1] // 3
    return jnp.concatenate(
        [
            parts_ref[p, which * size : (which + 1) * size].astype(F32)[
                g * across : (g + 1) * across
            ]
            for p in range(count)
        ],
        0,
    ).astype(BF16)


def logits_kernel(across, core_ref, qkv_ref, own_ref, other_ref, q_ref, k_ref, sum_ref):
    for g in range(5):
        q_ref[:, g * LANES : (g + 1) * LANES] = gathered(qkv_ref, 0, g, across)
        k_ref[:, g * LANES : (g + 1) * LANES] = gathered(qkv_ref, 1, g, across)
    rows = 128
    for m in range(LENGTH // rows):
        sum_ref[m * rows : (m + 1) * rows, :] = lax.dot_general(
            q_ref[m * rows : (m + 1) * rows, :],
            k_ref[...],
            (((1,), (1,)), ((), ())),
            preferred_element_type=F32,
        )
    core = core_ref[0]
    own_ref[...] = sum_ref[pl.ds(pl.multiple_of(core * HALF, HALF), HALF), :]
    other_ref[...] = sum_ref[pl.ds(pl.multiple_of((1 - core) * HALF, HALF), HALF), :].astype(BF16)


def join_kernel(own_ref, other_ref, out_ref):
    out_ref[OWNERS:] = jnp.zeros((out_ref.shape[0] - OWNERS, BLOCK, LENGTH), BF16)
    total = own_ref[...] + other_ref[...].astype(F32)
    spare = jnp.zeros((OWNERS * BLOCK - HALF, LENGTH), F32)
    total = jnp.concatenate([total, spare], 0)
    for m in range(OWNERS):
        out_ref[m] = total[m * BLOCK : (m + 1) * BLOCK].astype(BF16)


def bias_kernel(weight_ref, near_ref, far_ref, out_ref):
    bins = 64
    near, far = near_ref[...], far_ref[...]
    square = jnp.zeros((BLOCK, LENGTH), F32)
    for c in range(3):
        off = near[:, c : c + 1] - far[c : c + 1, :]
        square = square + off * off
    width = bins / RADIAL_REACH
    spacing = length_of(square) * width

    def some(at, total):
        for u in range(8):
            b = at * 8 + u
            away = spacing - b.astype(F32) * (width * RADIAL_REACH / (bins - 1))
            total = total + weight_ref[b] * jnp.exp(-(away * away))
        return total

    out_ref[...] = lax.fori_loop(0, bins // 8, some, jnp.zeros((BLOCK, LENGTH), F32))


def softmax_kernel(parts_ref, bias_ref, out_ref):
    count = parts_ref.shape[0]
    logits = bias_ref[...]
    for p in range(count):
        logits = logits + parts_ref[p].astype(F32)
    scaled = jnp.exp(logits - jnp.max(logits, axis=-1, keepdims=True))
    weights = (scaled / jnp.sum(scaled, axis=-1, keepdims=True)).astype(BF16)
    for p in range(count):
        out_ref[p] = weights


def mix_kernel(across, core_ref, own_ref, other_ref, parts_ref, out_ref, a_ref, v_ref):
    core = core_ref[0]
    for ref, half in ((own_ref, core), (other_ref, 1 - core)):
        rows = jnp.concatenate([ref[m].astype(F32) for m in range(OWNERS)], 0)[:HALF]
        a_ref[pl.ds(pl.multiple_of(half * HALF, HALF), HALF), :] = rows.astype(BF16)
    for g in range(5):
        v_ref[:, g * LANES : (g + 1) * LANES] = gathered(parts_ref, 2, g, across)
    rows = 160
    for m in range(LENGTH // rows):
        mixed = dot(a_ref[m * rows : (m + 1) * rows, :], v_ref[...])
        for p in range(rows // across):
            pieces = [
                mixed[p * across : (p + 1) * across, g * LANES : (g + 1) * LANES]
                for g in range(5)
            ]
            spare = out_ref.shape[1] - 5 * across
            if spare:
                pieces.append(jnp.zeros((spare, LANES), F32))
            out_ref[m * (rows // across) + p] = jnp.concatenate(pieces, 0).astype(BF16)


def column_start_kernel(
    x_ref, gate_ref, mixed_ref, mask_ref, gain_ref, weights_ref,
    new_ref, qkv_ref, turned_ref, z_ref, wide_out_ref, wide_ref,
):
    widen_out(weights_ref[3 * CH :, :], wide_out_ref)
    for at in range(3):
        widen(weights_ref[at * CH : (at + 1) * CH, :], wide_ref, at * HEADS * LANES)
    norm_gain = gain_ref[...]
    for s in range(2):
        gated = jnp.concatenate(
            [
                (gate_ref[h, s].astype(F32) * mixed_ref[h * 2 + s].astype(F32)).astype(BF16)
                for h in range(HEADS)
            ],
            1,
        )
        update = dot(gated, wide_out_ref[...])
        for g in range(5):
            rows = []
            for i in range(4):
                n = (s * 5 + g) * 4 + i
                part = update[g * COLS : (g + 1) * COLS, i * CH : (i + 1) * CH]
                rows.append((x_ref[n].astype(F32) + part).astype(BF16))
                new_ref[n] = rows[-1]
            z = normed(jnp.concatenate(rows, 0), norm_gain)
            first = (s * 5 + g) * 4 * COLS
            z_ref[first : first + 4 * COLS, :] = z
    for chunk in range(4):
        pieces, masks = [], []
        for g in range(5):
            column = (chunk * 5 + g) * 4
            pieces.append(
                jnp.concatenate(
                    [z_ref[pl.ds(column + i, ROWS, stride=COLS), :] for i in range(4)], 1
                )
            )
            masks.append(spread_mask(mask_ref[...], chunk * 5 + g))

        size = qkv_ref.shape[1] // 3
        z = jnp.concatenate(pieces, 0)
        spare = size - z.shape[0]
        z = jnp.concatenate([z, jnp.zeros((spare, z.shape[1]), F32)], 0).astype(BF16)
        turned_ref[chunk] = z
        mask = jnp.concatenate(masks + [jnp.zeros((spare, LANES), F32)], 0)

        def put(matrix, h, one):
            qkv_ref[h * 4 + chunk, matrix * size : (matrix + 1) * size] = one.astype(BF16)

        put_projections(z, mask, wide_ref, put)


def finish_kernel(x_ref, gate_ref, mixed_ref, wo_ref, out_ref, turned_ref, wide_out_ref):
    widen_out(wo_ref[...], wide_out_ref)
    for chunk in range(4):
        gated = jnp.concatenate(
            [
                gate_ref[h, chunk].astype(F32) * mixed_ref[h * 4 + chunk].astype(F32)
                for h in range(HEADS)
            ],
            1,
        ).astype(BF16)
        update = dot(gated, wide_out_ref[...])
        for g in range(5):
            for i in range(4):
                column = (chunk * 5 + g) * 4 + i
                turned_ref[pl.ds(column, ROWS, stride=COLS), :] = update[
                    g * ROWS : (g + 1) * ROWS, i * CH : (i + 1) * CH
                ]
    for n in range(ROWS):
        out_ref[n] = (x_ref[n].astype(F32) + turned_ref[n * COLS : (n + 1) * COLS, :]).astype(BF16)


def exchange(parts, axes):
    return lax.all_to_all(parts, axes, split_axis=0, concat_axis=0, tiled=True)


def swap_cores(x):
    return lax.ppermute(x, "core", [(0, 1), (1, 0)])


def column_tokens(mine, cols_n):
    device = lambda r, c: r * cols_n + c
    half = cols_n
    rows_n = 2 * cols_n
    ways = []
    for flip in (0, 1):
        pairs = [
            (device(r, c), device(c + half * ((r % 2) ^ flip), r // 2))
            for r in range(rows_n)
            for c in range(cols_n)
        ]
        ways.append(lax.ppermute(mine, EVERYWHERE, pairs))
    return ways


def tied_attention(across, qkv, core, bias, sum_axes, pass_axes, beside):
    own, other = call(
        functools.partial(logits_kernel, across),
        (shape((HALF, LENGTH), F32), shape((HALF, LENGTH), BF16)),
        [SMEM, VMEM],
        [
            pltpu.VMEM((LENGTH, 5 * LANES), BF16),
            pltpu.VMEM((LENGTH, 5 * LANES), BF16),
            pltpu.VMEM((LENGTH, LENGTH), F32),
        ],
    )(core, qkv)
    parts = call(join_kernel, shape((16, BLOCK, LENGTH), BF16), [VMEM] * 2)(own, swap_cores(other))
    parts = exchange(parts, sum_axes)
    weights = call(softmax_kernel, shape((16, BLOCK, LENGTH), BF16), [VMEM] * 2)(
        parts, bias
    )
    own, first = lax.optimization_barrier((exchange(weights, sum_axes)[:OWNERS], beside[0]))
    other = swap_cores(own)
    mixed = call(
        functools.partial(mix_kernel, across),
        shape((qkv.shape[0], 5 * across + 5 * across % 16, LANES), BF16),
        [SMEM, VMEM, VMEM, VMEM],
        [pltpu.VMEM((LENGTH, LENGTH), BF16), pltpu.VMEM((LENGTH, 5 * LANES), BF16)],
    )(core, own, other, qkv)
    mixed, second = lax.optimization_barrier((exchange(mixed, pass_axes), beside[1]))
    return mixed, first, second


def shards(
    pair, pair_mask, node_state, coords, neighbours, atom_type, type_table, node_query, node_key,
    node_value, edge_pair, edge_radial, node_out_w, coord_gain, radial_pair, row_gain, row_query,
    row_key, row_value, row_gate, row_out, row_bias, column_gain, column_query, column_key,
    column_value, column_gate, column_out, column_bias,
):
    rows_n, cols_n, channels = pair.shape
    row, col = lax.axis_index(("x", "y")), lax.axis_index(("z", "core"))
    core = lax.axis_index("core")[None].astype(jnp.int32)
    node_width = node_state.shape[1]
    onehot = (atom_type[:, None] == jnp.arange(type_table.shape[0], dtype=jnp.int32)[None, :])
    features = node_state + jnp.dot(onehot.astype(F32), type_table, precision=PRECISE)
    spare = LANES - node_width
    near = jnp.concatenate(
        [features, coords.T, jnp.zeros((rows_n, spare - coords.shape[0]), F32)], 1
    )
    ways = column_tokens(near, 8)
    place = jnp.stack([col * cols_n, (row < 8).astype(jnp.int32)]).astype(jnp.int32)
    remote = (pair, neighbours, node_query, node_key, node_value, edge_pair, edge_radial)
    small, sums = call(
        graph_kernel,
        (shape((128, 8, LANES), F32), shape((48, LANES), BF16)),
        [SMEM] * 2 + [VMEM] * 10,
        [pltpu.VMEM((ROWS, LANES), F32)] * 2,
        limit=60,
    )(place, coords, near, *ways, *remote)
    small, *weights = lax.optimization_barrier((small, row_query, row_key, row_value))
    weights = jnp.concatenate(weights, 0)
    small = exchange(small, EVERYWHERE)
    updated = call(merge_kernel, shape((16, 8, LANES), F32), [SMEM, VMEM])(coord_gain, small)
    place = jnp.stack([col, core[0], row]).astype(jnp.int32)

    groups = ROWS // 4
    projected = lambda count, size: [
        shape((ROWS, COLS, CH), BF16),
        shape((count, size, LANES), BF16),
    ]
    x, qkv, z = call(
        row_start_kernel,
        (*projected(8, 3 * 400 + 48), shape((2, 400, 4 * CH), BF16)),
        [SMEM] * 2 + [VMEM] * 7,
        [
            pltpu.VMEM((4 * CH, 3 * HEADS * LANES), BF16),
        ],
    )(
        place, updated, updated, sums, pair, pair_mask.T.astype(BF16), radial_pair, row_gain[None],
        weights,
    )

    qkv = exchange(qkv, ("z", "core"))
    all_xyz = updated[:, :, :15].reshape(16, 8, 5, 3).transpose(3, 0, 2, 1).reshape(3, LENGTH)
    new_coords = lax.dynamic_slice_in_dim(all_xyz, row * rows_n, rows_n, 1)
    new_state = call(
        node_kernel, shape((ROWS, node_width), F32), [SMEM] + [VMEM] * 4
    )(place, small, qkv, near, node_out_w)
    more_xyz = jnp.pad(all_xyz, ((0, 0), (0, OWNERS * BLOCK - HALF)))

    def gate(z, weight):
        return call(
            gate_kernel,
            shape((HEADS,) + z.shape[:2] + (LANES,), BF16),
            [VMEM] * 2,
            [pltpu.VMEM((4 * CH, HEADS * LANES), BF16)],
        )(z, weight)

    def bias(weight, head, place):
        first = core[0] * HALF + jnp.minimum(place, OWNERS - 1) * BLOCK
        tokens = lax.dynamic_slice_in_dim(more_xyz, first, BLOCK, 1).T
        return call(bias_kernel, shape((BLOCK, LENGTH), F32), [SMEM, VMEM, VMEM])(
            lax.dynamic_index_in_dim(weight, head, 1, keepdims=False), tokens, all_xyz
        )

    row_biases = bias(row_bias, lax.axis_index("z"), row)
    column_biases = bias(column_bias, lax.axis_index("x"), lax.axis_index(("y", "z")))
    qkv, *weights = lax.optimization_barrier(
        (qkv, column_query, column_key, column_value, row_out)
    )
    weights = jnp.concatenate(weights, 0)
    mixed, (new_state, new_coords), row_gates = tied_attention(
        COLS, qkv, core, row_biases, ("x", "y"), ("z", "core"),
        ((new_state, new_coords), gate(z, row_gate)),
    )
    x, qkv, z = call(
        column_start_kernel,
        (*projected(16, 3 * 208), shape((4, 208, 4 * CH), BF16)),
        [VMEM] * 6,
        [
            pltpu.VMEM((ROWS * COLS, CH), F32),
            pltpu.VMEM((HEADS * LANES, 4 * CH), BF16),
            pltpu.VMEM((4 * CH, 3 * HEADS * LANES), BF16),
        ],
    )(
        x, row_gates, mixed, pair_mask.astype(BF16), column_gain[None], weights,
    )
    mixed, _, column_gates = tied_attention(
        ROWS, exchange(qkv, ("x", "y")), core, column_biases, ("y", "z"), ("x", "y"),
        ((), gate(z, column_gate)),
    )
    pair_out = call(
        finish_kernel,
        shape((ROWS, COLS, CH), BF16),
        [VMEM] * 4,
        [
            pltpu.VMEM((ROWS * COLS, CH), F32),
            pltpu.VMEM((HEADS * LANES, 4 * CH), BF16),
        ],
    )(x, column_gates, mixed, column_out)
    return (pair_out, new_state, new_coords)


def solution(mesh):
    cube = Mesh(mesh.devices.reshape(4, 4, 4, 2), EVERYWHERE)
    row, col = ("x", "y"), ("z", "core")
    placed = (
        P(row, col, None), P(row, col), P(row, None), P(None, row), P(row, None), P(row),
    ) + (P(),) * 23
    return jax.shard_map(
        shards,
        mesh=cube,
        in_specs=placed,
        out_specs=(P(row, col, None), P(row, None), P(None, row)),
        check_vma=False,
    )
```

time: 280 us -> 252 us (0.900)
  blocking collectives: 153 us -> 85.1 us
  waiting for transfers between devices: 38 us -> 69.2 us
  starting transfers between devices: 33 us -> 41.8 us
  Pallas kernels: 38.5 us -> 35.6 us
    all_to_all x5 -> x3, blocking collectives: 126 us -> 85.1 us  [exchange(): return lax.all_to_all(parts, axes, split_axis=0, concat_axis=0, tiled=True)]
    all_to_all x4 -> x6, waiting for transfers between devices: 29.8 us -> 61.3 us  [exchange(): return lax.all_to_all(parts, axes, split_axis=0, concat_axis=0, tiled=True)]
    all_gather x1 -> x0, blocking collectives: 27.1 us -> none  [shards(): all_xyz = lax.all_gather(new_coords, ('x', 'y'), axis=1, tiled=True)]
    all_to_all x4 -> x6, starting transfers between devices: 18.1 us -> 32.5 us  [exchange(): return lax.all_to_all(parts, axes, split_axis=0, concat_axis=0, tiled=True)]
    ppermute x4 -> x2, starting transfers between devices: 14.6 us -> 8.9 us  [column_tokens(): ways.append(lax.ppermute(mine, EVERYWHERE, pairs))]
    pallas_call x6 -> x9, Pallas kernels: 27.3 us -> 25.6 us  [the longest x1 6.82 us: shards(): call(row_start_kernel, (*projected(8, 3 * 400 + 48), shape((2, 400, 4 * C...]
    unnamed x63 -> x57, local copies, waits for them, and re-layouts: 6.72 us -> 6.32 us
  transfers between devices with their start and end apart: 12 -> 12, of which waited for: 8 -> 11; matrix products, arithmetic and copies ran while one was open for 2% -> 4% of each run, Pallas kernels for 1% -> 3%
where the time goes in v2:
time: 252 us; the launch traced here: 250 us
  blocking collectives  85.1 us (34%)
  waiting for transfers between devices  69.2 us (27%)
  starting transfers between devices  41.8 us (17%)
  Pallas kernels  35.6 us (14%)
  local copies, waits for them, and re-layouts  13.3 us (5%)
  other arithmetic  3.15 us (1%)
    all_to_all x3, blocking collectives, exchange(): return lax.all_to_all(parts, axes, split_axis=0, concat_axis=0, tiled=True)  85.1 us
    all_to_all x6, waiting for transfers between devices, exchange(): return lax.all_to_all(parts, axes, split_axis=0, concat_axis=0, tiled=True)  61.3 us
    all_to_all x6, starting transfers between devices, exchange(): return lax.all_to_all(parts, axes, split_axis=0, concat_axis=0, tiled=True)  32.5 us
    ppermute x2, starting transfers between devices, column_tokens(): ways.append(lax.ppermute(mine, EVERYWHERE, pairs))  8.9 us
    ppermute x4, waiting for transfers between devices, swap_cores(): return lax.ppermute(x, 'core', [(0, 1), (1, 0)])  6.99 us
    pallas_call x1, Pallas kernels, shards(): call(row_start_kernel, (*projected(8, 3 * 400 + 48), shape((2, 400, 4 * C...  6.82 us
    unnamed x57, local copies, waits for them, and re-layouts  6.32 us
    pallas_call x1, Pallas kernels, shards(): call(graph_kernel, (shape((128, 8, LANES), F32), shape((48, LANES), BF16)...  6.16 us
  transfers between devices with their start and end apart: 12, of which 11 were waited for; matrix products, arithmetic and copies ran while one was open for 4% of the time, Pallas kernels for 3%

profile of v2, /device:TPU:0, one launch (start us, length us, event | category | flops | bytes accessed | tf_op | source)
XLA Modules:
  0.0 250.2 jit_solution(12064390480959594672)
XLA Ops:
  3.3 8.2 %collective-permute-start.1 = (f32[40,128]{1,0:T(8,128)S(1)}, f32[40,128]{1,0:T(8,128)S(1)}, u32[]{:S(2)}, u32[]{:S(2)}) collective-permute-start(f32[40,128]{1,0:T(8,128)S(1)} %maximum_maximum_fusion.near_ref), channel_id=1, source_target_pairs={{0,64},{1,72},{2,80},{3,88},{4,96},{5,104},{6,112},{7,120},{8,0},{... | collective-permute-start | bytes 61448 | tf_op jit(solution)/shard_map/ppermute | solution.py:534
  13.7 6.2 %shard_map.292 = (f32[128,8,128]{2,1,0:T(8,128)}, bf16[48,128]{1,0:T(8,128)(2,1)}) custom-call(s32[2]{0:T(128)} %pad_add_fusion.1.place_ref, f32[3,40]{1,0:T(4,128)} %xyz_ref.1, f32[40,128]{1,0:T(8,128)} %copy-done.13, f32[40,128]{1,0:T(8,128)} %copy-done.26, f32[40,128]{1,0:T(8,128)} %copy-done.27, bf16[40,80,128]{2,1,0:T(8,128)(2,1)} %pair_ref.3, ...), custom_call_target="tpu_custom_call" | custom-call | tf_op jit(solution)/shard_map/pallas_call | solution.py:585
  19.8 12.8 %all-to-all-start = ((f32[128,8,128]{2,1,0:T(8,128)}), f32[128,8,128]{2,1,0:T(8,128)S(1)}, u32[]{:S(2)}, u32[]{:S(2)}) async-start(f32[128,8,128]{2,1,0:T(8,128)} %get-tuple-element.32), calls=%async_computation | async-start | bytes 1048576 | tf_op jit(solution)/shard_map/all_to_all | solution.py:516
  34.3 12.0 %all-to-all-done.parts_ref = f32[128,8,128]{2,1,0:T(8,128)S(1)} async-done(((f32[128,8,128]{2,1,0:T(8,128)}), f32[128,8,128]{2,1,0:T(8,128)S(1)}, u32[]{:S(2)}, u32[]{:S(2)}) %all-to-all-start) | async-done | bytes 524320 | tf_op jit(solution)/shard_map/all_to_all | solution.py:516
  48.7 6.8 %shard_map.294 = (bf16[40,80,128]{2,1,0:T(8,128)(2,1)S(1)}, bf16[8,1248,128]{2,1,0:T(8,128)(2,1)S(1)}, bf16[2,400,512]{2,1,0:T(8,128)(2,1)S(1)}) custom-call(s32[3]{0:T(128)S(1)} %pad_add_fusion.place_ref, f32[16,8,128]{2,1,0:T(8,128)S(1)} %shard_map.293.xyz_ref.new_ref, f32[16,8,128]{2,1,0:T(8,128)S(1)} %shard_map.293.xyz_ref.new_ref, ...), custom_call_target="tpu_custom_call" | custom-call | tf_op jit(solution)/shard_map/pallas_call | solution.py:603
  56.4 34.9 %all_to_all.45.qkv_ref.sent_ref.parts_ref = bf16[8,1248,128]{2,1,0:T(8,128)(2,1)S(1)} all-to-all(bf16[8,1248,128]{2,1,0:T(8,128)(2,1)S(1)} %get-tuple-element.38), channel_id=1, replica_groups=mesh['x'=4,'y'=4,'z'=4,'core'=2] {'z','core'}, dimensions={0} | all-to-all | bytes 5111808 | tf_op jit(solution)/shard_map/all_to_all | solution.py:516
  95.6 4.4 %all-to-all-start.2 = ((bf16[16,24,640]{2,1,0:T(8,128)(2,1)}), bf16[16,24,640]{2,1,0:T(8,128)(2,1)}, u32[]{:S(2)}, u32[]{:S(2)}) async-start(bf16[16,24,640]{2,1,0:T(8,128)(2,1)} %copy-done.3), calls=%async_computation.2 | async-start | bytes 983040 | tf_op jit(solution)/shard_map/all_to_all | solution.py:516
  106.1 5.6 %all-to-all-done.2.parts_ref = bf16[16,24,640]{2,1,0:T(8,128)(2,1)} async-done(((bf16[16,24,640]{2,1,0:T(8,128)(2,1)}), bf16[16,24,640]{2,1,0:T(8,128)(2,1)}, u32[]{:S(2)}, u32[]{:S(2)}) %all-to-all-start.2) | async-done | bytes 491552 | tf_op jit(solution)/shard_map/all_to_all | solution.py:516
  113.8 4.2 %all-to-all-start.3 = ((bf16[16,24,640]{2,1,0:T(8,128)(2,1)}), bf16[16,24,640]{2,1,0:T(8,128)(2,1)}, u32[]{:S(2)}, u32[]{:S(2)}) async-start(bf16[16,24,640]{2,1,0:T(8,128)(2,1)} %copy-done.2), calls=%async_computation.3 | async-start | bytes 983040 | tf_op jit(solution)/shard_map/all_to_all | solution.py:516
  118.7 1.8 shard_map.299
  120.5 7.6 %all-to-all-done.3 = bf16[16,24,640]{2,1,0:T(8,128)(2,1)} async-done(((bf16[16,24,640]{2,1,0:T(8,128)(2,1)}), bf16[16,24,640]{2,1,0:T(8,128)(2,1)}, u32[]{:S(2)}, u32[]{:S(2)}) %all-to-all-start.3) | async-done | bytes 491552 | tf_op jit(solution)/shard_map/all_to_all | solution.py:516
  131.0 2.0 shard_map.300
  133.0 3.9 %all-to-all-start.4 = ((bf16[8,400,128]{2,1,0:T(8,128)(2,1)}), bf16[8,400,128]{2,1,0:T(8,128)(2,1)S(1)}, u32[]{:S(2)}, u32[]{:S(2)}) async-start(bf16[8,400,128]{2,1,0:T(8,128)(2,1)} %shard_map.300), calls=%async_computation.4 | async-start | bytes 1638400 | tf_op jit(solution)/shard_map/all_to_all | solution.py:516
  138.5 11.7 %all-to-all-done.4.mixed_ref = bf16[8,400,128]{2,1,0:T(8,128)(2,1)S(1)} async-done(((bf16[8,400,128]{2,1,0:T(8,128)(2,1)}), bf16[8,400,128]{2,1,0:T(8,128)(2,1)S(1)}, u32[]{:S(2)}, u32[]{:S(2)}) %all-to-all-start.4) | async-done | bytes 819232 | tf_op jit(solution)/shard_map/all_to_all | solution.py:516
  150.1 3.7 %shard_map.302 = (bf16[40,80,128]{2,1,0:T(8,128)(2,1)S(1)}, bf16[16,624,128]{2,1,0:T(8,128)(2,1)S(1)}, bf16[4,208,512]{2,1,0:T(8,128)(2,1)S(1)}) custom-call(bf16[40,80,128]{2,1,0:T(8,128)(2,1)S(1)} %copy-done.8, bf16[4,2,400,128]{3,2,1,0:T(8,128)(2,1)S(1)} %shard_map.301.gate_ref, bf16[8,400,128]{2,1,0:T(8,128)(2,1)S(1)} %all-to-all-done.4.mixed_ref, ...), custom_call_target="tpu_custom_call" | custom-call | tf_op jit(solution)/shard_map/pallas_call | solution.py:648
  154.7 36.3 %all_to_all.46.qkv_ref.parts_ref = bf16[16,624,128]{2,1,0:T(8,128)(2,1)S(1)} all-to-all(bf16[16,624,128]{2,1,0:T(8,128)(2,1)S(1)} %get-tuple-element.51), channel_id=1, replica_groups=mesh['x'=4,'y'=4,'z'=4,'core'=2] {'x','y'}, dimensions={0} | all-to-all | bytes 5111808 | tf_op jit(solution)/shard_map/all_to_all | solution.py:516
  195.2 3.6 %all-to-all-start.6 = ((bf16[16,24,640]{2,1,0:T(8,128)(2,1)}), bf16[16,24,640]{2,1,0:T(8,128)(2,1)S(1)}, u32[]{:S(2)}, u32[]{:S(2)}) async-start(bf16[16,24,640]{2,1,0:T(8,128)(2,1)} %copy-done.4), calls=%async_computation.6 | async-start | bytes 983040 | tf_op jit(solution)/shard_map/all_to_all | solution.py:516
  201.2 9.3 %all-to-all-done.6.parts_ref = bf16[16,24,640]{2,1,0:T(8,128)(2,1)S(1)} async-done(((bf16[16,24,640]{2,1,0:T(8,128)(2,1)}), bf16[16,24,640]{2,1,0:T(8,128)(2,1)S(1)}, u32[]{:S(2)}, u32[]{:S(2)}) %all-to-all-start.6) | async-done | bytes 491552 | tf_op jit(solution)/shard_map/all_to_all | solution.py:516
  210.8 13.9 %all_to_all.47 = bf16[16,24,640]{2,1,0:T(8,128)(2,1)S(1)} all-to-all(bf16[16,24,640]{2,1,0:T(8,128)(2,1)S(1)} %shard_map.306), channel_id=1, replica_groups=mesh['x'=4,'y'=4,'z'=4,'core'=2] {'y','z'}, dimensions={0} | all-to-all | bytes 983040 | tf_op jit(solution)/shard_map/all_to_all | solution.py:516
  224.8 1.8 collective-permute-done.5.other_ref
  226.6 2.0 shard_map.307
  228.6 3.8 %all-to-all-start.8 = ((bf16[16,208,128]{2,1,0:T(8,128)(2,1)}), bf16[16,208,128]{2,1,0:T(8,128)(2,1)S(1)}, u32[]{:S(2)}, u32[]{:S(2)}) async-start(bf16[16,208,128]{2,1,0:T(8,128)(2,1)} %shard_map.307), calls=%async_computation.8 | async-start | bytes 1703936 | tf_op jit(solution)/shard_map/all_to_all | solution.py:516
  233.1 15.2 %all-to-all-done.8.mixed_ref = bf16[16,208,128]{2,1,0:T(8,128)(2,1)S(1)} async-done(((bf16[16,208,128]{2,1,0:T(8,128)(2,1)}), bf16[16,208,128]{2,1,0:T(8,128)(2,1)S(1)}, u32[]{:S(2)}, u32[]{:S(2)}) %all-to-all-start.8) | async-done | bytes 852000 | tf_op jit(solution)/shard_map/all_to_all | solution.py:516
  248.3 1.9 shard_map.309
  (99 shorter events, 35.6 us)
Async XLA Ops:
  0.6 47.3 %copy-start.1 = (bf16[40,80,128]{2,1,0:T(8,128)(2,1)S(1)}, bf16[40,80,128]{2,1,0:T(8,128)(2,1)}, u32[]{:S(2)}) copy-start(bf16[40,80,128]{2,1,0:T(8,128)(2,1)} %pair_ref.3) | copy-start | bytes 2457604
  0.7 45.7 %copy-start.23 = (f32[4]{0:T(128)S(1)}, f32[4]{0:T(128)}, u32[]{:S(2)}) copy-start(f32[4]{0:T(128)} %gain_ref.1) | copy-start | bytes 52
  0.7 47.3 %copy-start.21 = (f32[128]{0:T(128)S(1)}, f32[128]{0:T(128)}, u32[]{:S(2)}) copy-start(f32[128]{0:T(128)} %param.44) | copy-start | bytes 1540
  0.7 47.3 %copy-start.17 = (f32[64,128]{1,0:T(8,128)S(1)}, f32[64,128]{1,0:T(8,128)}, u32[]{:S(2)}) copy-start(f32[64,128]{1,0:T(8,128)} %radial_ref.1) | copy-start | bytes 98308
  2.7 9.6 %collective-permute-start = (f32[40,128]{1,0:T(8,128)S(1)}, f32[40,128]{1,0:T(8,128)S(1)}, u32[]{:S(2)}, u32[]{:S(2)}) collective-permute-start(f32[40,128]{1,0:T(8,128)S(1)} %maximum_maximum_fusion.near_ref), channel_id=1, source_target_pairs={{0,0},{1,8},{2,16},{3,24},{4,32},{5,40},{6,48},{7,56},{8,64},{9,72... | collective-permute-start | bytes 61448 | tf_op jit(solution)/shard_map/ppermute | solution.py:534
  3.3 9.7 %collective-permute-start.1 = (f32[40,128]{1,0:T(8,128)S(1)}, f32[40,128]{1,0:T(8,128)S(1)}, u32[]{:S(2)}, u32[]{:S(2)}) collective-permute-start(f32[40,128]{1,0:T(8,128)S(1)} %maximum_maximum_fusion.near_ref), channel_id=1, source_target_pairs={{0,64},{1,72},{2,80},{3,88},{4,96},{5,104},{6,112},{7,120},{8,0},{... | collective-permute-start | bytes 61448 | tf_op jit(solution)/shard_map/ppermute | solution.py:534
  19.8 26.5 %all-to-all-start = ((f32[128,8,128]{2,1,0:T(8,128)}), f32[128,8,128]{2,1,0:T(8,128)S(1)}, u32[]{:S(2)}, u32[]{:S(2)}) async-start(f32[128,8,128]{2,1,0:T(8,128)} %get-tuple-element.32), calls=%async_computation | async-start | bytes 1048576 | tf_op jit(solution)/shard_map/all_to_all | solution.py:516
  56.4 34.9 %copy-start.9 = (bf16[2,400,512]{2,1,0:T(8,128)(2,1)}, bf16[2,400,512]{2,1,0:T(8,128)(2,1)S(1)}, u32[]{:S(2)}) copy-start(bf16[2,400,512]{2,1,0:T(8,128)(2,1)S(1)} %get-tuple-element.43.z_ref) | copy-start | bytes 2457604
  92.9 1.8 collective-permute-start.2
  95.6 23.1 %copy-start.14 = (f32[40,128]{1,0:T(8,128)S(1)}, f32[40,128]{1,0:T(8,128)}, u32[]{:S(2)}) copy-start(f32[40,128]{1,0:T(8,128)} %copy-done.13) | copy-start | bytes 61444
  95.6 23.1 %copy-start.15 = (f32[64,64]{1,0:T(8,128)S(1)}, f32[64,64]{1,0:T(8,128)}, u32[]{:S(2)}) copy-start(f32[64,64]{1,0:T(8,128)} %wo_ref.2) | copy-start | bytes 49156
  95.6 16.1 %all-to-all-start.2 = ((bf16[16,24,640]{2,1,0:T(8,128)(2,1)}), bf16[16,24,640]{2,1,0:T(8,128)(2,1)}, u32[]{:S(2)}, u32[]{:S(2)}) async-start(bf16[16,24,640]{2,1,0:T(8,128)(2,1)} %copy-done.3), calls=%async_computation.2 | async-start | bytes 983040 | tf_op jit(solution)/shard_map/all_to_all | solution.py:516
  113.8 14.3 %all-to-all-start.3 = ((bf16[16,24,640]{2,1,0:T(8,128)(2,1)}), bf16[16,24,640]{2,1,0:T(8,128)(2,1)}, u32[]{:S(2)}, u32[]{:S(2)}) async-start(bf16[16,24,640]{2,1,0:T(8,128)(2,1)} %copy-done.2), calls=%async_computation.3 | async-start | bytes 983040 | tf_op jit(solution)/shard_map/all_to_all | solution.py:516
  129.1 1.9 collective-permute-start.3
  133.0 17.1 %copy-start.8 = (bf16[40,80,128]{2,1,0:T(8,128)(2,1)S(1)}, bf16[40,80,128]{2,1,0:T(8,128)(2,1)}, u32[]{:S(2)}) copy-start(bf16[40,80,128]{2,1,0:T(8,128)(2,1)} %copy-done.7) | copy-start | bytes 2457604
  133.0 17.1 %copy-start.22 = (f32[128]{0:T(128)S(1)}, f32[128]{0:T(128)}, u32[]{:S(2)}) copy-start(f32[128]{0:T(128)} %param.51) | copy-start | bytes 1540
  133.0 17.1 %all-to-all-start.4 = ((bf16[8,400,128]{2,1,0:T(8,128)(2,1)}), bf16[8,400,128]{2,1,0:T(8,128)(2,1)S(1)}, u32[]{:S(2)}, u32[]{:S(2)}) async-start(bf16[8,400,128]{2,1,0:T(8,128)(2,1)} %shard_map.300), calls=%async_computation.4 | async-start | bytes 1638400 | tf_op jit(solution)/shard_map/all_to_all | solution.py:516
  154.7 36.3 %copy-start.5 = (bf16[4,208,512]{2,1,0:T(8,128)(2,1)}, bf16[4,208,512]{2,1,0:T(8,128)(2,1)S(1)}, u32[]{:S(2)}) copy-start(bf16[4,208,512]{2,1,0:T(8,128)(2,1)S(1)} %get-tuple-element.54.z_ref) | copy-start | bytes 2555908
  192.6 1.8 collective-permute-start.4
  195.2 15.3 %all-to-all-start.6 = ((bf16[16,24,640]{2,1,0:T(8,128)(2,1)}), bf16[16,24,640]{2,1,0:T(8,128)(2,1)S(1)}, u32[]{:S(2)}, u32[]{:S(2)}) async-start(bf16[16,24,640]{2,1,0:T(8,128)(2,1)} %copy-done.4), calls=%async_computation.6 | async-start | bytes 983040 | tf_op jit(solution)/shard_map/all_to_all | solution.py:516
  224.7 1.9 collective-permute-start.5
  228.6 19.7 %copy-start.12 = (bf16[40,80,128]{2,1,0:T(8,128)(2,1)S(1)}, bf16[40,80,128]{2,1,0:T(8,128)(2,1)}, u32[]{:S(2)}) copy-start(bf16[40,80,128]{2,1,0:T(8,128)(2,1)} %copy-done.11) | copy-start | bytes 2457604
  228.6 19.7 %copy-start.16 = (bf16[128,128]{1,0:T(8,128)(2,1)S(1)}, bf16[128,128]{1,0:T(8,128)(2,1)}, u32[]{:S(2)}) copy-start(bf16[128,128]{1,0:T(8,128)(2,1)} %wo_ref.3) | copy-start | bytes 98308
  228.6 19.7 %all-to-all-start.8 = ((bf16[16,208,128]{2,1,0:T(8,128)(2,1)}), bf16[16,208,128]{2,1,0:T(8,128)(2,1)S(1)}, u32[]{:S(2)}, u32[]{:S(2)}) async-start(bf16[16,208,128]{2,1,0:T(8,128)(2,1)} %shard_map.307), calls=%async_computation.8 | async-start | bytes 1703936 | tf_op jit(solution)/shard_map/all_to_all | solution.py:516
  (16 other events, 60.9 us)

commit v3 on v2

--- a/solution.py
+++ b/solution.py
@@ -149,7 +149,7 @@
         sums_ref[pl.ds(first, step), :] = jnp.concatenate(sums, 0)
         return jnp.where(lane // 24 == block, jnp.concatenate(lines, 0), small)
 
-    small = lax.fori_loop(0, ROWS // step, some, jnp.zeros((step, LANES), F32))
+    small = lax.fori_loop(0, ROWS // step, some, jnp.zeros((step, LANES), F32), unroll=True)
     small_ref[...] = jnp.broadcast_to(small[None], small_ref.shape)
     sums = sums_ref[...]
     turned = pltpu.roll(sums, 64, 1)
@@ -331,7 +331,7 @@
         return carry
 
     groups = ROWS // 4
-    lax.fori_loop(0, groups // together, some, 0)
+    lax.fori_loop(0, groups // together, some, 0, unroll=True)
     for s in range(2):
         for h in range(HEADS):
             qkv_ref[h * 2 + s, 3 * size :] = sums_ref[...]
@@ -388,9 +388,31 @@
         out_ref[m] = total[m * BLOCK : (m + 1) * BLOCK].astype(BF16)
 
 
-def bias_kernel(weight_ref, near_ref, far_ref, out_ref):
+def turned_dot(a, b):
+    return sum(
+        lax.dot_general(a, part, (((1,), (1,)), ((), ())), preferred_element_type=F32)
+        for part in split3(b)
+    )
+
+
+def places_kernel(new_ref, out_ref):
+    flat = new_ref[...].reshape(LANES, LANES)
+    sides = []
+    for g in range(5):
+        pick = (iota((8, LANES), 1) == iota((8, LANES), 0) + 3 * g) & (iota((8, LANES), 0) < 3)
+        sides.append(turned_dot(jnp.where(pick, 1.0, 0.0).astype(BF16), flat))
+    parts = jnp.concatenate(split3(jnp.concatenate(sides, 1)), 0)
+    at, token = iota((LENGTH, LENGTH), 0), iota((LENGTH, LENGTH), 1)
+    target = (at & 127) // 8 * ROWS + at // LANES * 8 + (at & 7)
+    moved = dot(parts, jnp.where(target == token, 1.0, 0.0).astype(BF16))
+    out_ref[...] = moved[:8] + moved[8:16] + moved[16:]
+
+
+def bias_kernel(place_ref, weight_ref, far_ref, out_ref):
     bins = 64
-    near, far = near_ref[...], far_ref[...]
+    far = far_ref[...]
+    pick = iota((BLOCK, LENGTH), 1) == iota((BLOCK, LENGTH), 0) + place_ref[1]
+    near = turned_dot(jnp.where(pick, 1.0, 0.0).astype(BF16), far)
     square = jnp.zeros((BLOCK, LENGTH), F32)
     for c in range(3):
         off = near[:, c : c + 1] - far[c : c + 1, :]
@@ -402,7 +424,7 @@
         for u in range(8):
             b = at * 8 + u
             away = spacing - b.astype(F32) * (width * RADIAL_REACH / (bins - 1))
-            total = total + weight_ref[b] * jnp.exp(-(away * away))
+            total = total + weight_ref[b, place_ref[0]] * jnp.exp(-(away * away))
         return total
 
     out_ref[...] = lax.fori_loop(0, bins // 8, some, jnp.zeros((BLOCK, LENGTH), F32))
@@ -547,11 +569,11 @@
         ],
     )(core, qkv)
     parts = call(join_kernel, shape((16, BLOCK, LENGTH), BF16), [VMEM] * 2)(own, swap_cores(other))
-    parts = exchange(parts, sum_axes)
+    parts, beside = lax.optimization_barrier((exchange(parts, sum_axes), beside))
     weights = call(softmax_kernel, shape((16, BLOCK, LENGTH), BF16), [VMEM] * 2)(
         parts, bias
     )
-    own, first = lax.optimization_barrier((exchange(weights, sum_axes)[:OWNERS], beside[0]))
+    own = exchange(weights, sum_axes)
     other = swap_cores(own)
     mixed = call(
         functools.partial(mix_kernel, across),
@@ -559,8 +581,7 @@
         [SMEM, VMEM, VMEM, VMEM],
         [pltpu.VMEM((LENGTH, LENGTH), BF16), pltpu.VMEM((LENGTH, 5 * LANES), BF16)],
     )(core, own, other, qkv)
-    mixed, second = lax.optimization_barrier((exchange(mixed, pass_axes), beside[1]))
-    return mixed, first, second
+    return exchange(mixed, pass_axes), beside
 
 
 def shards(
@@ -613,13 +634,11 @@
     )
 
     qkv = exchange(qkv, ("z", "core"))
-    all_xyz = updated[:, :, :15].reshape(16, 8, 5, 3).transpose(3, 0, 2, 1).reshape(3, LENGTH)
-    new_coords = lax.dynamic_slice_in_dim(all_xyz, row * rows_n, rows_n, 1)
+    all_xyz = call(places_kernel, shape((8, LENGTH), F32), [VMEM])(updated)
+    new_coords = lax.dynamic_slice(all_xyz, (0, row * rows_n), (3, rows_n))
     new_state = call(
         node_kernel, shape((ROWS, node_width), F32), [SMEM] + [VMEM] * 4
     )(place, small, qkv, near, node_out_w)
-    more_xyz = jnp.pad(all_xyz, ((0, 0), (0, OWNERS * BLOCK - HALF)))
-
     def gate(z, weight):
         return call(
             gate_kernel,
@@ -628,11 +647,10 @@
             [pltpu.VMEM((4 * CH, HEADS * LANES), BF16)],
         )(z, weight)
 
-    def bias(weight, head, place):
-        first = core[0] * HALF + jnp.minimum(place, OWNERS - 1) * BLOCK
-        tokens = lax.dynamic_slice_in_dim(more_xyz, first, BLOCK, 1).T
-        return call(bias_kernel, shape((BLOCK, LENGTH), F32), [SMEM, VMEM, VMEM])(
-            lax.dynamic_index_in_dim(weight, head, 1, keepdims=False), tokens, all_xyz
+    def bias(weight, head, owner):
+        first = core[0] * HALF + jnp.minimum(owner, OWNERS - 1) * BLOCK
+        return call(bias_kernel, shape((BLOCK, LENGTH), F32), [SMEM, SMEM, VMEM])(
+            jnp.stack([head, first]).astype(jnp.int32), weight, all_xyz
         )
 
     row_biases = bias(row_bias, lax.axis_index("z"), row)
@@ -641,9 +659,9 @@
         (qkv, column_query, column_key, column_value, row_out)
     )
     weights = jnp.concatenate(weights, 0)
-    mixed, (new_state, new_coords), row_gates = tied_attention(
+    mixed, (new_state, new_coords, row_gates) = tied_attention(
         COLS, qkv, core, row_biases, ("x", "y"), ("z", "core"),
-        ((new_state, new_coords), gate(z, row_gate)),
+        (new_state, new_coords, gate(z, row_gate)),
     )
     x, qkv, z = call(
         column_start_kernel,
@@ -657,9 +675,9 @@
     )(
         x, row_gates, mixed, pair_mask.astype(BF16), column_gain[None], weights,
     )
-    mixed, _, column_gates = tied_attention(
+    mixed, column_gates = tied_attention(
         ROWS, exchange(qkv, ("x", "y")), core, column_biases, ("y", "z"), ("x", "y"),
-        ((), gate(z, column_gate)),
+        gate(z, column_gate),
     )
     pair_out = call(
         finish_kernel,

time: 252 us -> 248 us (0.984)
  blocking collectives: 85.1 us -> 118 us
  waiting for transfers between devices: 69.2 us -> 42.9 us
  starting transfers between devices: 41.8 us -> 34.1 us
  local copies, waits for them, and re-layouts: 13.3 us -> 10.2 us
    all_to_all x3 -> x5, blocking collectives: 85.1 us -> 118 us  [exchange(): return lax.all_to_all(parts, axes, split_axis=0, concat_axis=0, tiled=True)]
    all_to_all x6 -> x4, waiting for transfers between devices: 61.3 us -> 34.9 us  [exchange(): return lax.all_to_all(parts, axes, split_axis=0, concat_axis=0, tiled=True)]
    all_to_all x6 -> x4, starting transfers between devices: 32.5 us -> 25 us  [exchange(): return lax.all_to_all(parts, axes, split_axis=0, concat_axis=0, tiled=True)]
    unnamed x57 -> x67, local copies, waits for them, and re-layouts: 6.32 us -> 9.33 us
    pallas_call x2 -> x3, Pallas kernels: 3.39 us -> 5.39 us  [the longest x2 4.78 us: bias(): call(bias_kernel, shape((BLOCK, LENGTH), F32), [SMEM, SMEM, VMEM])]
  transfers between devices with their start and end apart: 12 -> 10, of which waited for: 11 -> 9; matrix products, arithmetic and copies ran while one was open for 4% -> 2% of each run, Pallas kernels for 3% -> 4%
where the time goes in v3:
time: 248 us; the launch traced here: 247 us
  blocking collectives  118 us (48%)
  waiting for transfers between devices  42.9 us (17%)
  Pallas kernels  36.2 us (15%)
  starting transfers between devices  34.1 us (14%)
  local copies, waits for them, and re-layouts  10.2 us (4%)
  other arithmetic  3.27 us (1%)
    all_to_all x5, blocking collectives, exchange(): return lax.all_to_all(parts, axes, split_axis=0, concat_axis=0, tiled=True)  118 us
    all_to_all x4, waiting for transfers between devices, exchange(): return lax.all_to_all(parts, axes, split_axis=0, concat_axis=0, tiled=True)  34.9 us
    all_to_all x4, starting transfers between devices, exchange(): return lax.all_to_all(parts, axes, split_axis=0, concat_axis=0, tiled=True)  25 us
    unnamed x67, local copies, waits for them, and re-layouts  9.33 us
    ppermute x2, starting transfers between devices, column_tokens(): ways.append(lax.ppermute(mine, EVERYWHERE, pairs))  8.9 us
    ppermute x4, waiting for transfers between devices, swap_cores(): return lax.ppermute(x, 'core', [(0, 1), (1, 0)])  7.18 us
    pallas_call x1, Pallas kernels, shards(): call(graph_kernel, (shape((128, 8, LANES), F32), shape((48, LANES), BF16)...  5.58 us
    pallas_call x1, Pallas kernels, shards(): call(row_start_kernel, (*projected(8, 3 * 400 + 48), shape((2, 400, 4 * C...  5.01 us
  transfers between devices with their start and end apart: 10, of which 9 were waited for; matrix products, arithmetic and copies ran while one was open for 2% of the time, Pallas kernels for 4%

profile of v3, /device:TPU:0, one launch (start us, length us, event | category | flops | bytes accessed | tf_op | source)
XLA Modules:
  0.0 246.7 jit_solution(906555356494748599)
XLA Ops:
  3.3 8.2 %collective-permute-start.1 = (f32[40,128]{1,0:T(8,128)S(1)}, f32[40,128]{1,0:T(8,128)S(1)}, u32[]{:S(2)}, u32[]{:S(2)}) collective-permute-start(f32[40,128]{1,0:T(8,128)S(1)} %maximum_maximum_fusion.near_ref), channel_id=1, source_target_pairs={{0,64},{1,72},{2,80},{3,88},{4,96},{5,104},{6,112},{7,120},{8,0},{... | collective-permute-start | bytes 61448 | tf_op jit(solution)/shard_map/ppermute | solution.py:556
  13.7 5.6 %shard_map.292 = (f32[128,8,128]{2,1,0:T(8,128)}, bf16[48,128]{1,0:T(8,128)(2,1)}) custom-call(s32[2]{0:T(128)} %pad_add_fusion.1.place_ref, f32[3,40]{1,0:T(4,128)} %xyz_ref.1, f32[40,128]{1,0:T(8,128)} %copy-done.13, f32[40,128]{1,0:T(8,128)} %copy-done.28, f32[40,128]{1,0:T(8,128)} %copy-done.29, bf16[40,80,128]{2,1,0:T(8,128)(2,1)} %pair_ref.3, ...), custom_call_target="tpu_custom_call" | custom-call | tf_op jit(solution)/shard_map/pallas_call | solution.py:606
  19.2 12.8 %all-to-all-start = ((f32[128,8,128]{2,1,0:T(8,128)}), f32[128,8,128]{2,1,0:T(8,128)S(1)}, u32[]{:S(2)}, u32[]{:S(2)}) async-start(f32[128,8,128]{2,1,0:T(8,128)} %get-tuple-element.31), calls=%async_computation | async-start | bytes 1048576 | tf_op jit(solution)/shard_map/all_to_all | solution.py:538
  33.8 12.0 %all-to-all-done.parts_ref = f32[128,8,128]{2,1,0:T(8,128)S(1)} async-done(((f32[128,8,128]{2,1,0:T(8,128)}), f32[128,8,128]{2,1,0:T(8,128)S(1)}, u32[]{:S(2)}, u32[]{:S(2)}) %all-to-all-start) | async-done | bytes 524320 | tf_op jit(solution)/shard_map/all_to_all | solution.py:538
  48.1 5.0 %shard_map.294 = (bf16[40,80,128]{2,1,0:T(8,128)(2,1)S(1)}, bf16[8,1248,128]{2,1,0:T(8,128)(2,1)S(1)}, bf16[2,400,512]{2,1,0:T(8,128)(2,1)S(1)}) custom-call(s32[3]{0:T(128)S(1)} %pad_add_fusion.place_ref, f32[16,8,128]{2,1,0:T(8,128)S(1)} %shard_map.293.xyz_ref.new_ref, f32[16,8,128]{2,1,0:T(8,128)S(1)} %shard_map.293.xyz_ref.new_ref, ...), custom_call_target="tpu_custom_call" | custom-call | tf_op jit(solution)/shard_map/pallas_call | solution.py:624
  54.0 34.9 %all_to_all.45.qkv_ref.sent_ref.parts_ref = bf16[8,1248,128]{2,1,0:T(8,128)(2,1)S(1)} all-to-all(bf16[8,1248,128]{2,1,0:T(8,128)(2,1)S(1)} %get-tuple-element.37), channel_id=1, replica_groups=mesh['x'=4,'y'=4,'z'=4,'core'=2] {'z','core'}, dimensions={0} | all-to-all | bytes 5111808 | tf_op jit(solution)/shard_map/all_to_all | solution.py:538
  93.2 4.4 %all-to-all-start.2 = ((bf16[16,24,640]{2,1,0:T(8,128)(2,1)}), bf16[16,24,640]{2,1,0:T(8,128)(2,1)}, u32[]{:S(2)}, u32[]{:S(2)}) async-start(bf16[16,24,640]{2,1,0:T(8,128)(2,1)} %copy-done.4), calls=%async_computation.2 | async-start | bytes 983040 | tf_op jit(solution)/shard_map/all_to_all | solution.py:538
  101.3 2.4 shard_map.300.bias_ref
  104.3 1.8 shard_map.297
  106.2 3.1 %all-to-all-done.2.parts_ref = bf16[16,24,640]{2,1,0:T(8,128)(2,1)} async-done(((bf16[16,24,640]{2,1,0:T(8,128)(2,1)}), bf16[16,24,640]{2,1,0:T(8,128)(2,1)}, u32[]{:S(2)}, u32[]{:S(2)}) %all-to-all-start.2) | async-done | bytes 491552 | tf_op jit(solution)/shard_map/all_to_all | solution.py:538
  110.5 14.8 %all_to_all.46.own_ref = bf16[16,24,640]{2,1,0:T(8,128)(2,1)S(1)} all-to-all(bf16[16,24,640]{2,1,0:T(8,128)(2,1)S(1)} %shard_map.301), channel_id=1, replica_groups=mesh['x'=4,'y'=4,'z'=4,'core'=2] {'x','y'}, dimensions={0} | all-to-all | bytes 983040 | tf_op jit(solution)/shard_map/all_to_all | solution.py:538
  125.5 1.9 collective-permute-done.3.other_ref
  127.3 2.0 shard_map.302
  129.3 3.5 %all-to-all-start.4 = ((bf16[8,400,128]{2,1,0:T(8,128)(2,1)}), bf16[8,400,128]{2,1,0:T(8,128)(2,1)S(1)}, u32[]{:S(2)}, u32[]{:S(2)}) async-start(bf16[8,400,128]{2,1,0:T(8,128)(2,1)} %shard_map.302), calls=%async_computation.4 | async-start | bytes 1638400 | tf_op jit(solution)/shard_map/all_to_all | solution.py:538
  133.7 12.6 %all-to-all-done.4.mixed_ref = bf16[8,400,128]{2,1,0:T(8,128)(2,1)S(1)} async-done(((bf16[8,400,128]{2,1,0:T(8,128)(2,1)}), bf16[8,400,128]{2,1,0:T(8,128)(2,1)S(1)}, u32[]{:S(2)}, u32[]{:S(2)}) %all-to-all-start.4) | async-done | bytes 819232 | tf_op jit(solution)/shard_map/all_to_all | solution.py:538
  147.5 3.7 %shard_map.303 = (bf16[40,80,128]{2,1,0:T(8,128)(2,1)S(1)}, bf16[16,624,128]{2,1,0:T(8,128)(2,1)S(1)}, bf16[4,208,512]{2,1,0:T(8,128)(2,1)S(1)}) custom-call(bf16[40,80,128]{2,1,0:T(8,128)(2,1)S(1)} %copy-done.8, bf16[4,2,400,128]{3,2,1,0:T(8,128)(2,1)S(1)} %copy-done.2, bf16[8,400,128]{2,1,0:T(8,128)(2,1)S(1)} %all-to-all-done.4.mixed_ref, ...), custom_call_target="tpu_custom_call" | custom-call | tf_op jit(solution)/shard_map/pallas_call | solution.py:666
  152.1 36.3 %all_to_all.47.qkv_ref.parts_ref = bf16[16,624,128]{2,1,0:T(8,128)(2,1)S(1)} all-to-all(bf16[16,624,128]{2,1,0:T(8,128)(2,1)S(1)} %get-tuple-element.49), channel_id=1, replica_groups=mesh['x'=4,'y'=4,'z'=4,'core'=2] {'x','y'}, dimensions={0} | all-to-all | bytes 5111808 | tf_op jit(solution)/shard_map/all_to_all | solution.py:538
  192.6 4.2 %all-to-all-start.6 = ((bf16[16,24,640]{2,1,0:T(8,128)(2,1)}), bf16[16,24,640]{2,1,0:T(8,128)(2,1)}, u32[]{:S(2)}, u32[]{:S(2)}) async-start(bf16[16,24,640]{2,1,0:T(8,128)(2,1)} %shard_map.305), calls=%async_computation.6 | async-start | bytes 983040 | tf_op jit(solution)/shard_map/all_to_all | solution.py:538
  197.1 2.4 shard_map.307.bias_ref
  201.4 7.2 %all-to-all-done.6.parts_ref = bf16[16,24,640]{2,1,0:T(8,128)(2,1)} async-done(((bf16[16,24,640]{2,1,0:T(8,128)(2,1)}), bf16[16,24,640]{2,1,0:T(8,128)(2,1)}, u32[]{:S(2)}, u32[]{:S(2)}) %all-to-all-start.6) | async-done | bytes 491552 | tf_op jit(solution)/shard_map/all_to_all | solution.py:538
  209.9 13.9 %all_to_all.48.own_ref = bf16[16,24,640]{2,1,0:T(8,128)(2,1)S(1)} all-to-all(bf16[16,24,640]{2,1,0:T(8,128)(2,1)S(1)} %shard_map.308), channel_id=1, replica_groups=mesh['x'=4,'y'=4,'z'=4,'core'=2] {'y','z'}, dimensions={0} | all-to-all | bytes 983040 | tf_op jit(solution)/shard_map/all_to_all | solution.py:538
  223.8 1.9 collective-permute-done.5.other_ref
  226.7 18.0 %all_to_all.49.mixed_ref = bf16[16,208,128]{2,1,0:T(8,128)(2,1)S(1)} all-to-all(bf16[16,208,128]{2,1,0:T(8,128)(2,1)S(1)} %shard_map.309), channel_id=1, replica_groups=mesh['x'=4,'y'=4,'z'=4,'core'=2] {'x','y'}, dimensions={0} | all-to-all | bytes 1703936 | tf_op jit(solution)/shard_map/all_to_all | solution.py:538
  244.7 1.9 shard_map.310
  (101 shorter events, 30.9 us)
Async XLA Ops:
  0.6 46.7 %copy-start.3 = (bf16[40,80,128]{2,1,0:T(8,128)(2,1)S(1)}, bf16[40,80,128]{2,1,0:T(8,128)(2,1)}, u32[]{:S(2)}) copy-start(bf16[40,80,128]{2,1,0:T(8,128)(2,1)} %pair_ref.3) | copy-start | bytes 2457604
  0.7 45.1 %copy-start.23 = (f32[4]{0:T(128)S(1)}, f32[4]{0:T(128)}, u32[]{:S(2)}) copy-start(f32[4]{0:T(128)} %gain_ref.1) | copy-start | bytes 52
  0.7 46.7 %copy-start.21 = (f32[128]{0:T(128)S(1)}, f32[128]{0:T(128)}, u32[]{:S(2)}) copy-start(f32[128]{0:T(128)} %param.44) | copy-start | bytes 1540
  0.7 46.7 %copy-start.17 = (f32[64,128]{1,0:T(8,128)S(1)}, f32[64,128]{1,0:T(8,128)}, u32[]{:S(2)}) copy-start(f32[64,128]{1,0:T(8,128)} %radial_ref.1) | copy-start | bytes 98308
  2.7 10.4 %copy-start.13 = (f32[40,128]{1,0:T(8,128)}, f32[40,128]{1,0:T(8,128)S(1)}, u32[]{:S(2)}) copy-start(f32[40,128]{1,0:T(8,128)S(1)} %maximum_maximum_fusion.near_ref) | copy-start | bytes 61444
  2.7 9.6 %collective-permute-start = (f32[40,128]{1,0:T(8,128)S(1)}, f32[40,128]{1,0:T(8,128)S(1)}, u32[]{:S(2)}, u32[]{:S(2)}) collective-permute-start(f32[40,128]{1,0:T(8,128)S(1)} %maximum_maximum_fusion.near_ref), channel_id=1, source_target_pairs={{0,0},{1,8},{2,16},{3,24},{4,32},{5,40},{6,48},{7,56},{8,64},{9,72... | collective-permute-start | bytes 61448 | tf_op jit(solution)/shard_map/ppermute | solution.py:556
  3.3 9.7 %collective-permute-start.1 = (f32[40,128]{1,0:T(8,128)S(1)}, f32[40,128]{1,0:T(8,128)S(1)}, u32[]{:S(2)}, u32[]{:S(2)}) collective-permute-start(f32[40,128]{1,0:T(8,128)S(1)} %maximum_maximum_fusion.near_ref), channel_id=1, source_target_pairs={{0,64},{1,72},{2,80},{3,88},{4,96},{5,104},{6,112},{7,120},{8,0},{... | collective-permute-start | bytes 61448 | tf_op jit(solution)/shard_map/ppermute | solution.py:556
  19.2 26.5 %all-to-all-start = ((f32[128,8,128]{2,1,0:T(8,128)}), f32[128,8,128]{2,1,0:T(8,128)S(1)}, u32[]{:S(2)}, u32[]{:S(2)}) async-start(f32[128,8,128]{2,1,0:T(8,128)} %get-tuple-element.31), calls=%async_computation | async-start | bytes 1048576 | tf_op jit(solution)/shard_map/all_to_all | solution.py:538
  54.0 34.9 %copy-start.11 = (bf16[2,400,512]{2,1,0:T(8,128)(2,1)}, bf16[2,400,512]{2,1,0:T(8,128)(2,1)S(1)}, u32[]{:S(2)}) copy-start(bf16[2,400,512]{2,1,0:T(8,128)(2,1)S(1)} %get-tuple-element.41.z_ref) | copy-start | bytes 2457604
  90.5 13.8 %copy-start.14 = (f32[40,128]{1,0:T(8,128)S(1)}, f32[40,128]{1,0:T(8,128)}, u32[]{:S(2)}) copy-start(f32[40,128]{1,0:T(8,128)} %copy-done.13) | copy-start | bytes 61444
  90.5 13.8 %copy-start.15 = (f32[64,64]{1,0:T(8,128)S(1)}, f32[64,64]{1,0:T(8,128)}, u32[]{:S(2)}) copy-start(f32[64,64]{1,0:T(8,128)} %wo_ref.2) | copy-start | bytes 49156
  90.5 1.8 collective-permute-start.2
  93.2 16.0 %all-to-all-start.2 = ((bf16[16,24,640]{2,1,0:T(8,128)(2,1)}), bf16[16,24,640]{2,1,0:T(8,128)(2,1)}, u32[]{:S(2)}, u32[]{:S(2)}) async-start(bf16[16,24,640]{2,1,0:T(8,128)(2,1)} %copy-done.4), calls=%async_computation.2 | async-start | bytes 983040 | tf_op jit(solution)/shard_map/all_to_all | solution.py:538
  125.3 21.0 %copy-start.2 = (bf16[4,2,400,128]{3,2,1,0:T(8,128)(2,1)S(1)}, bf16[4,2,400,128]{3,2,1,0:T(8,128)(2,1)}, u32[]{:S(2)}) copy-start(bf16[4,2,400,128]{3,2,1,0:T(8,128)(2,1)} %copy-done.1) | copy-start | bytes 2457604
  125.4 21.0 %copy-start.22 = (f32[128]{0:T(128)S(1)}, f32[128]{0:T(128)}, u32[]{:S(2)}) copy-start(f32[128]{0:T(128)} %param.51) | copy-start | bytes 1540
  125.4 1.9 collective-permute-start.3
  129.3 17.0 %all-to-all-start.4 = ((bf16[8,400,128]{2,1,0:T(8,128)(2,1)}), bf16[8,400,128]{2,1,0:T(8,128)(2,1)S(1)}, u32[]{:S(2)}, u32[]{:S(2)}) async-start(bf16[8,400,128]{2,1,0:T(8,128)(2,1)} %shard_map.302), calls=%async_computation.4 | async-start | bytes 1638400 | tf_op jit(solution)/shard_map/all_to_all | solution.py:538
  152.1 36.3 %copy-start.5 = (bf16[4,208,512]{2,1,0:T(8,128)(2,1)}, bf16[4,208,512]{2,1,0:T(8,128)(2,1)S(1)}, u32[]{:S(2)}) copy-start(bf16[4,208,512]{2,1,0:T(8,128)(2,1)S(1)} %get-tuple-element.52.z_ref) | copy-start | bytes 2555908
  188.4 11.0 %copy-start.19 = (bf16[128,128]{1,0:T(8,128)(2,1)S(1)}, bf16[128,128]{1,0:T(8,128)(2,1)}, u32[]{:S(2)}) copy-start(bf16[128,128]{1,0:T(8,128)(2,1)} %weight_ref.5) | copy-start | bytes 98308
  190.0 1.8 collective-permute-start.4
  192.6 16.0 %all-to-all-start.6 = ((bf16[16,24,640]{2,1,0:T(8,128)(2,1)}), bf16[16,24,640]{2,1,0:T(8,128)(2,1)}, u32[]{:S(2)}, u32[]{:S(2)}) async-start(bf16[16,24,640]{2,1,0:T(8,128)(2,1)} %shard_map.305), calls=%async_computation.6 | async-start | bytes 983040 | tf_op jit(solution)/shard_map/all_to_all | solution.py:538
  223.8 21.0 %copy-start.10 = (bf16[40,80,128]{2,1,0:T(8,128)(2,1)S(1)}, bf16[40,80,128]{2,1,0:T(8,128)(2,1)}, u32[]{:S(2)}) copy-start(bf16[40,80,128]{2,1,0:T(8,128)(2,1)} %copy-done.9) | copy-start | bytes 2457604
  223.8 21.0 %copy-start.16 = (bf16[128,128]{1,0:T(8,128)(2,1)S(1)}, bf16[128,128]{1,0:T(8,128)(2,1)}, u32[]{:S(2)}) copy-start(bf16[128,128]{1,0:T(8,128)(2,1)} %wo_ref.3) | copy-start | bytes 98308
  223.8 1.9 collective-permute-start.5
  (18 other events, 67.0 us)

commit v4 on v3

--- a/solution.py
+++ b/solution.py
@@ -379,15 +379,6 @@
     other_ref[...] = sum_ref[pl.ds(pl.multiple_of((1 - core) * HALF, HALF), HALF), :].astype(BF16)
 
 
-def join_kernel(own_ref, other_ref, out_ref):
-    out_ref[OWNERS:] = jnp.zeros((out_ref.shape[0] - OWNERS, BLOCK, LENGTH), BF16)
-    total = own_ref[...] + other_ref[...].astype(F32)
-    spare = jnp.zeros((OWNERS * BLOCK - HALF, LENGTH), F32)
-    total = jnp.concatenate([total, spare], 0)
-    for m in range(OWNERS):
-        out_ref[m] = total[m * BLOCK : (m + 1) * BLOCK].astype(BF16)
-
-
 def turned_dot(a, b):
     return sum(
         lax.dot_general(a, part, (((1,), (1,)), ((), ())), preferred_element_type=F32)
@@ -544,12 +535,11 @@
 
 def column_tokens(mine, cols_n):
     device = lambda r, c: r * cols_n + c
-    half = cols_n
     rows_n = 2 * cols_n
     ways = []
     for flip in (0, 1):
         pairs = [
-            (device(r, c), device(c + half * ((r % 2) ^ flip), r // 2))
+            (device(r, c), device(2 * c + ((r % 2) ^ flip), r // 2))
             for r in range(rows_n)
             for c in range(cols_n)
         ]
@@ -568,7 +558,8 @@
             pltpu.VMEM((LENGTH, LENGTH), F32),
         ],
     )(core, qkv)
-    parts = call(join_kernel, shape((16, BLOCK, LENGTH), BF16), [VMEM] * 2)(own, swap_cores(other))
+    parts = (own + swap_cores(other).astype(F32)).astype(BF16)
+    parts = jnp.pad(parts, ((0, 16 * BLOCK - HALF), (0, 0))).reshape(16, BLOCK, LENGTH)
     parts, beside = lax.optimization_barrier((exchange(parts, sum_axes), beside))
     weights = call(softmax_kernel, shape((16, BLOCK, LENGTH), BF16), [VMEM] * 2)(
         parts, bias
@@ -601,7 +592,7 @@
         [features, coords.T, jnp.zeros((rows_n, spare - coords.shape[0]), F32)], 1
     )
     ways = column_tokens(near, 8)
-    place = jnp.stack([col * cols_n, (row < 8).astype(jnp.int32)]).astype(jnp.int32)
+    place = jnp.stack([col * cols_n, (row % 2 == 0).astype(jnp.int32)]).astype(jnp.int32)
     remote = (pair, neighbours, node_query, node_key, node_value, edge_pair, edge_radial)
     small, sums = call(
         graph_kernel,

time: 248 us -> 248 us (level)
    ppermute x2, starting transfers between devices: 8.9 us -> 2.39 us  [column_tokens(): ways.append(lax.ppermute(mine, EVERYWHERE, pairs))]
    all_to_all x4, starting transfers between devices: 25 us -> 31.4 us  [exchange(): return lax.all_to_all(parts, axes, split_axis=0, concat_axis=0, tiled=True)]
    unnamed x67 -> x65, local copies, waits for them, and re-layouts: 9.33 us -> 8.53 us
where the time goes in v4:
time: 248 us; the launch traced here: 247 us
  blocking collectives  118 us (48%)
  waiting for transfers between devices  43.6 us (18%)
  Pallas kernels  35.2 us (14%)
  starting transfers between devices  34 us (14%)
  local copies, waits for them, and re-layouts  11 us (4%)
  other arithmetic  3.4 us (1%)
    all_to_all x5, blocking collectives, exchange(): return lax.all_to_all(parts, axes, split_axis=0, concat_axis=0, tiled=True)  118 us
    all_to_all x4, waiting for transfers between devices, exchange(): return lax.all_to_all(parts, axes, split_axis=0, concat_axis=0, tiled=True)  34.9 us
    all_to_all x4, starting transfers between devices, exchange(): return lax.all_to_all(parts, axes, split_axis=0, concat_axis=0, tiled=True)  31.4 us
    unnamed x65, local copies, waits for them, and re-layouts  8.53 us
    ppermute x4, waiting for transfers between devices, swap_cores(): return lax.ppermute(x, 'core', [(0, 1), (1, 0)])  7.18 us
    pallas_call x1, Pallas kernels, shards(): call(graph_kernel, (shape((128, 8, LANES), F32), shape((48, LANES), BF16)...  5.56 us
    pallas_call x1, Pallas kernels, shards(): call(row_start_kernel, (*projected(8, 3 * 400 + 48), shape((2, 400, 4 * C...  5.01 us
  transfers between devices with their start and end apart: 10, of which 9 were waited for; matrix products, arithmetic and copies ran while one was open for 2% of the time, Pallas kernels for 4%

profile of v4, /device:TPU:0, one launch (start us, length us, event | category | flops | bytes accessed | tf_op | source)
XLA Modules:
  0.0 247.2 jit_solution(10079706182004725857)
XLA Ops:
  3.3 1.7 collective-permute-start.1
  7.8 5.6 %shard_map.292 = (f32[128,8,128]{2,1,0:T(8,128)}, bf16[48,128]{1,0:T(8,128)(2,1)}) custom-call(s32[2]{0:T(128)} %pad_add_fusion.1.place_ref, f32[3,40]{1,0:T(4,128)} %xyz_ref.1, f32[40,128]{1,0:T(8,128)} %copy-done.12, f32[40,128]{1,0:T(8,128)} %copy-done.27, f32[40,128]{1,0:T(8,128)} %copy-done.28, bf16[40,80,128]{2,1,0:T(8,128)(2,1)} %pair_ref.3, ...), custom_call_target="tpu_custom_call" | custom-call | tf_op jit(solution)/shard_map/pallas_call | solution.py:597
  13.3 19.2 %all-to-all-start = ((f32[128,8,128]{2,1,0:T(8,128)}), f32[128,8,128]{2,1,0:T(8,128)S(1)}, u32[]{:S(2)}, u32[]{:S(2)}) async-start(f32[128,8,128]{2,1,0:T(8,128)} %get-tuple-element.31), calls=%async_computation | async-start | bytes 1048576 | tf_op jit(solution)/shard_map/all_to_all | solution.py:529
  34.3 12.0 %all-to-all-done.parts_ref = f32[128,8,128]{2,1,0:T(8,128)S(1)} async-done(((f32[128,8,128]{2,1,0:T(8,128)}), f32[128,8,128]{2,1,0:T(8,128)S(1)}, u32[]{:S(2)}, u32[]{:S(2)}) %all-to-all-start) | async-done | bytes 524320 | tf_op jit(solution)/shard_map/all_to_all | solution.py:529
  48.7 5.0 %shard_map.294 = (bf16[40,80,128]{2,1,0:T(8,128)(2,1)S(1)}, bf16[8,1248,128]{2,1,0:T(8,128)(2,1)S(1)}, bf16[2,400,512]{2,1,0:T(8,128)(2,1)S(1)}) custom-call(s32[3]{0:T(128)S(1)} %pad_add_fusion.place_ref, f32[16,8,128]{2,1,0:T(8,128)S(1)} %shard_map.293.xyz_ref.new_ref, f32[16,8,128]{2,1,0:T(8,128)S(1)} %shard_map.293.xyz_ref.new_ref, ...), custom_call_target="tpu_custom_call" | custom-call | tf_op jit(solution)/shard_map/pallas_call | solution.py:615
  54.6 34.9 %all_to_all.45.qkv_ref.sent_ref.parts_ref = bf16[8,1248,128]{2,1,0:T(8,128)(2,1)S(1)} all-to-all(bf16[8,1248,128]{2,1,0:T(8,128)(2,1)S(1)} %get-tuple-element.37), channel_id=1, replica_groups=mesh['x'=4,'y'=4,'z'=4,'core'=2] {'z','core'}, dimensions={0} | all-to-all | bytes 5111808 | tf_op jit(solution)/shard_map/all_to_all | solution.py:529
  93.8 4.4 %all-to-all-start.2 = ((bf16[16,24,640]{2,1,0:T(8,128)(2,1)}), bf16[16,24,640]{2,1,0:T(8,128)(2,1)}, u32[]{:S(2)}, u32[]{:S(2)}) async-start(bf16[16,24,640]{2,1,0:T(8,128)(2,1)} %bitcast.19), calls=%async_computation.2 | async-start | bytes 983040 | tf_op jit(solution)/shard_map/all_to_all | solution.py:529
  101.8 2.4 shard_map.299.bias_ref
  104.9 1.8 shard_map.296
  106.7 3.1 %all-to-all-done.2.parts_ref = bf16[16,24,640]{2,1,0:T(8,128)(2,1)} async-done(((bf16[16,24,640]{2,1,0:T(8,128)(2,1)}), bf16[16,24,640]{2,1,0:T(8,128)(2,1)}, u32[]{:S(2)}, u32[]{:S(2)}) %all-to-all-start.2) | async-done | bytes 491552 | tf_op jit(solution)/shard_map/all_to_all | solution.py:529
  111.0 14.8 %all_to_all.46.own_ref = bf16[16,24,640]{2,1,0:T(8,128)(2,1)S(1)} all-to-all(bf16[16,24,640]{2,1,0:T(8,128)(2,1)S(1)} %shard_map.300), channel_id=1, replica_groups=mesh['x'=4,'y'=4,'z'=4,'core'=2] {'x','y'}, dimensions={0} | all-to-all | bytes 983040 | tf_op jit(solution)/shard_map/all_to_all | solution.py:529
  126.0 1.9 collective-permute-done.3.other_ref
  127.8 2.0 shard_map.301
  129.8 3.5 %all-to-all-start.4 = ((bf16[8,400,128]{2,1,0:T(8,128)(2,1)}), bf16[8,400,128]{2,1,0:T(8,128)(2,1)S(1)}, u32[]{:S(2)}, u32[]{:S(2)}) async-start(bf16[8,400,128]{2,1,0:T(8,128)(2,1)} %shard_map.301), calls=%async_computation.4 | async-start | bytes 1638400 | tf_op jit(solution)/shard_map/all_to_all | solution.py:529
  134.2 12.6 %all-to-all-done.4.mixed_ref = bf16[8,400,128]{2,1,0:T(8,128)(2,1)S(1)} async-done(((bf16[8,400,128]{2,1,0:T(8,128)(2,1)}), bf16[8,400,128]{2,1,0:T(8,128)(2,1)S(1)}, u32[]{:S(2)}, u32[]{:S(2)}) %all-to-all-start.4) | async-done | bytes 819232 | tf_op jit(solution)/shard_map/all_to_all | solution.py:529
  148.0 3.7 %shard_map.302 = (bf16[40,80,128]{2,1,0:T(8,128)(2,1)S(1)}, bf16[16,624,128]{2,1,0:T(8,128)(2,1)S(1)}, bf16[4,208,512]{2,1,0:T(8,128)(2,1)S(1)}) custom-call(bf16[40,80,128]{2,1,0:T(8,128)(2,1)S(1)} %copy-done.7, bf16[4,2,400,128]{3,2,1,0:T(8,128)(2,1)S(1)} %copy-done.2, bf16[8,400,128]{2,1,0:T(8,128)(2,1)S(1)} %all-to-all-done.4.mixed_ref, ...), custom_call_target="tpu_custom_call" | custom-call | tf_op jit(solution)/shard_map/pallas_call | solution.py:657
  152.6 36.4 %all_to_all.47.qkv_ref.parts_ref = bf16[16,624,128]{2,1,0:T(8,128)(2,1)S(1)} all-to-all(bf16[16,624,128]{2,1,0:T(8,128)(2,1)S(1)} %get-tuple-element.49), channel_id=1, replica_groups=mesh['x'=4,'y'=4,'z'=4,'core'=2] {'x','y'}, dimensions={0} | all-to-all | bytes 5111808 | tf_op jit(solution)/shard_map/all_to_all | solution.py:529
  193.2 4.2 %all-to-all-start.6 = ((bf16[16,24,640]{2,1,0:T(8,128)(2,1)}), bf16[16,24,640]{2,1,0:T(8,128)(2,1)}, u32[]{:S(2)}, u32[]{:S(2)}) async-start(bf16[16,24,640]{2,1,0:T(8,128)(2,1)} %bitcast.12), calls=%async_computation.6 | async-start | bytes 983040 | tf_op jit(solution)/shard_map/all_to_all | solution.py:529
  197.6 2.4 shard_map.305.bias_ref
  202.0 7.2 %all-to-all-done.6.parts_ref = bf16[16,24,640]{2,1,0:T(8,128)(2,1)} async-done(((bf16[16,24,640]{2,1,0:T(8,128)(2,1)}), bf16[16,24,640]{2,1,0:T(8,128)(2,1)}, u32[]{:S(2)}, u32[]{:S(2)}) %all-to-all-start.6) | async-done | bytes 491552 | tf_op jit(solution)/shard_map/all_to_all | solution.py:529
  210.5 13.9 %all_to_all.48.own_ref = bf16[16,24,640]{2,1,0:T(8,128)(2,1)S(1)} all-to-all(bf16[16,24,640]{2,1,0:T(8,128)(2,1)S(1)} %shard_map.306), channel_id=1, replica_groups=mesh['x'=4,'y'=4,'z'=4,'core'=2] {'y','z'}, dimensions={0} | all-to-all | bytes 983040 | tf_op jit(solution)/shard_map/all_to_all | solution.py:529
  224.3 1.9 collective-permute-done.5.other_ref
  227.3 18.0 %all_to_all.49.mixed_ref = bf16[16,208,128]{2,1,0:T(8,128)(2,1)S(1)} all-to-all(bf16[16,208,128]{2,1,0:T(8,128)(2,1)S(1)} %shard_map.307), channel_id=1, replica_groups=mesh['x'=4,'y'=4,'z'=4,'core'=2] {'x','y'}, dimensions={0} | all-to-all | bytes 1703936 | tf_op jit(solution)/shard_map/all_to_all | solution.py:529
  245.3 1.9 shard_map.308
  (101 shorter events, 31.6 us)
Async XLA Ops:
  0.6 47.3 %copy-start.3 = (bf16[40,80,128]{2,1,0:T(8,128)(2,1)S(1)}, bf16[40,80,128]{2,1,0:T(8,128)(2,1)}, u32[]{:S(2)}) copy-start(bf16[40,80,128]{2,1,0:T(8,128)(2,1)} %pair_ref.3) | copy-start | bytes 2457604
  0.7 45.6 %copy-start.22 = (f32[4]{0:T(128)S(1)}, f32[4]{0:T(128)}, u32[]{:S(2)}) copy-start(f32[4]{0:T(128)} %gain_ref.1) | copy-start | bytes 52
  0.7 47.3 %copy-start.20 = (f32[128]{0:T(128)S(1)}, f32[128]{0:T(128)}, u32[]{:S(2)}) copy-start(f32[128]{0:T(128)} %param.44) | copy-start | bytes 1540
  0.7 47.3 %copy-start.16 = (f32[64,128]{1,0:T(8,128)S(1)}, f32[64,128]{1,0:T(8,128)}, u32[]{:S(2)}) copy-start(f32[64,128]{1,0:T(8,128)} %radial_ref.1) | copy-start | bytes 98308
  2.7 3.0 %collective-permute-start = (f32[40,128]{1,0:T(8,128)S(1)}, f32[40,128]{1,0:T(8,128)S(1)}, u32[]{:S(2)}, u32[]{:S(2)}) collective-permute-start(f32[40,128]{1,0:T(8,128)S(1)} %maximum_maximum_fusion.near_ref), channel_id=1, source_target_pairs={{0,0},{1,16},{2,32},{3,48},{4,64},{5,80},{6,96},{7,112},{8,8},{9,2... | collective-permute-start | bytes 61448 | tf_op jit(solution)/shard_map/ppermute | solution.py:546
  3.3 3.9 %collective-permute-start.1 = (f32[40,128]{1,0:T(8,128)S(1)}, f32[40,128]{1,0:T(8,128)S(1)}, u32[]{:S(2)}, u32[]{:S(2)}) collective-permute-start(f32[40,128]{1,0:T(8,128)S(1)} %maximum_maximum_fusion.near_ref), channel_id=1, source_target_pairs={{0,8},{1,24},{2,40},{3,56},{4,72},{5,88},{6,104},{7,120},{8,0},{9,... | collective-permute-start | bytes 61448 | tf_op jit(solution)/shard_map/ppermute | solution.py:546
  13.3 33.0 %all-to-all-start = ((f32[128,8,128]{2,1,0:T(8,128)}), f32[128,8,128]{2,1,0:T(8,128)S(1)}, u32[]{:S(2)}, u32[]{:S(2)}) async-start(f32[128,8,128]{2,1,0:T(8,128)} %get-tuple-element.31), calls=%async_computation | async-start | bytes 1048576 | tf_op jit(solution)/shard_map/all_to_all | solution.py:529
  54.6 34.9 %copy-start.10 = (bf16[2,400,512]{2,1,0:T(8,128)(2,1)}, bf16[2,400,512]{2,1,0:T(8,128)(2,1)S(1)}, u32[]{:S(2)}) copy-start(bf16[2,400,512]{2,1,0:T(8,128)(2,1)S(1)} %get-tuple-element.41.z_ref) | copy-start | bytes 2457604
  89.5 9.5 %copy-start.17 = (bf16[128,128]{1,0:T(8,128)(2,1)S(1)}, bf16[128,128]{1,0:T(8,128)(2,1)}, u32[]{:S(2)}) copy-start(bf16[128,128]{1,0:T(8,128)(2,1)} %weight_ref.4) | copy-start | bytes 98308
  91.0 1.8 collective-permute-start.2
  92.9 12.0 %copy-start.13 = (f32[40,128]{1,0:T(8,128)S(1)}, f32[40,128]{1,0:T(8,128)}, u32[]{:S(2)}) copy-start(f32[40,128]{1,0:T(8,128)} %copy-done.12) | copy-start | bytes 61444
  92.9 12.0 %copy-start.14 = (f32[64,64]{1,0:T(8,128)S(1)}, f32[64,64]{1,0:T(8,128)}, u32[]{:S(2)}) copy-start(f32[64,64]{1,0:T(8,128)} %wo_ref.2) | copy-start | bytes 49156
  93.8 16.0 %all-to-all-start.2 = ((bf16[16,24,640]{2,1,0:T(8,128)(2,1)}), bf16[16,24,640]{2,1,0:T(8,128)(2,1)}, u32[]{:S(2)}, u32[]{:S(2)}) async-start(bf16[16,24,640]{2,1,0:T(8,128)(2,1)} %bitcast.19), calls=%async_computation.2 | async-start | bytes 983040 | tf_op jit(solution)/shard_map/all_to_all | solution.py:529
  125.9 21.0 %copy-start.2 = (bf16[4,2,400,128]{3,2,1,0:T(8,128)(2,1)S(1)}, bf16[4,2,400,128]{3,2,1,0:T(8,128)(2,1)}, u32[]{:S(2)}) copy-start(bf16[4,2,400,128]{3,2,1,0:T(8,128)(2,1)} %copy-done.1) | copy-start | bytes 2457604
  125.9 21.0 %copy-start.21 = (f32[128]{0:T(128)S(1)}, f32[128]{0:T(128)}, u32[]{:S(2)}) copy-start(f32[128]{0:T(128)} %param.51) | copy-start | bytes 1540
  125.9 1.9 collective-permute-start.3
  129.8 17.0 %all-to-all-start.4 = ((bf16[8,400,128]{2,1,0:T(8,128)(2,1)}), bf16[8,400,128]{2,1,0:T(8,128)(2,1)S(1)}, u32[]{:S(2)}, u32[]{:S(2)}) async-start(bf16[8,400,128]{2,1,0:T(8,128)(2,1)} %shard_map.301), calls=%async_computation.4 | async-start | bytes 1638400 | tf_op jit(solution)/shard_map/all_to_all | solution.py:529
  152.6 36.4 %copy-start.4 = (bf16[4,208,512]{2,1,0:T(8,128)(2,1)}, bf16[4,208,512]{2,1,0:T(8,128)(2,1)S(1)}, u32[]{:S(2)}) copy-start(bf16[4,208,512]{2,1,0:T(8,128)(2,1)S(1)} %get-tuple-element.52.z_ref) | copy-start | bytes 2555908
  189.0 11.1 %copy-start.18 = (bf16[128,128]{1,0:T(8,128)(2,1)S(1)}, bf16[128,128]{1,0:T(8,128)(2,1)}, u32[]{:S(2)}) copy-start(bf16[128,128]{1,0:T(8,128)(2,1)} %weight_ref.5) | copy-start | bytes 98308
  190.5 1.8 collective-permute-start.4
  193.2 16.0 %all-to-all-start.6 = ((bf16[16,24,640]{2,1,0:T(8,128)(2,1)}), bf16[16,24,640]{2,1,0:T(8,128)(2,1)}, u32[]{:S(2)}, u32[]{:S(2)}) async-start(bf16[16,24,640]{2,1,0:T(8,128)(2,1)} %bitcast.12), calls=%async_computation.6 | async-start | bytes 983040 | tf_op jit(solution)/shard_map/all_to_all | solution.py:529
  224.3 21.0 %copy-start.9 = (bf16[40,80,128]{2,1,0:T(8,128)(2,1)S(1)}, bf16[40,80,128]{2,1,0:T(8,128)(2,1)}, u32[]{:S(2)}) copy-start(bf16[40,80,128]{2,1,0:T(8,128)(2,1)} %copy-done.8) | copy-start | bytes 2457604
  224.3 21.0 %copy-start.15 = (bf16[128,128]{1,0:T(8,128)(2,1)S(1)}, bf16[128,128]{1,0:T(8,128)(2,1)}, u32[]{:S(2)}) copy-start(bf16[128,128]{1,0:T(8,128)(2,1)} %wo_ref.3) | copy-start | bytes 98308
  224.3 1.9 collective-permute-start.5
  (17 other events, 62.0 us)
